TPU v7x, 32 devices: a whole 2x2x4 slice. The times are simulated.
32 devices in a mesh: dp: 2 (over y), expert: 16 (over z, x, core).
Axes of the slice: x: 2, y: 2, z: 4, core: 2. Of those that a mesh axis runs over, the one named last changes fastest.
Arguments:
- tokens: bfloat16 [4096, 3584], P(('dp', 'expert')), may hold values from -6 to 6
- cotangent: bfloat16 [4096, 3584], P(('dp', 'expert')), may hold values from -0.59765625 to 0.59765625
- route_ids: int32 [4096, 8], P(('dp', 'expert')), may hold values from 0 to 383, as said below
- gates: bfloat16 [4096, 8], P(('dp', 'expert')), may hold values from 0.099609375 to 1
- w_gate: bfloat16 [16, 3584, 128], P('expert', None, 'dp'), may hold values from -0.09375 to 0.09375
- w_up: bfloat16 [16, 3584, 128], P('expert', None, 'dp'), may hold values from -0.09375 to 0.09375
- w_down: bfloat16 [16, 3584, 128], P('expert', None, 'dp'), may hold values from -0.125 to 0.125
Outputs:
- relaid_gate: bfloat16 [16, 3584, 128], P('expert', 'dp')
- relaid_up: bfloat16 [16, 3584, 128], P('expert', 'dp')
- relaid_down: bfloat16 [16, 3584, 128], P('expert', 'dp')
- grad_gate: float32 [16, 3584, 128], P('expert', 'dp')
- grad_up: float32 [16, 3584, 128], P('expert', 'dp')
- grad_down: float32 [16, 3584, 128], P('expert', 'dp')
- token_grad: bfloat16 [4096, 3584], P(('dp', 'expert'))
- gate_grad: float32 [4096, 8], P(('dp', 'expert'))
Inputs may be any that keep to these rules, and one draw needn't show every extreme that they name: `route_ids`: each row names 8 different experts. Among the 128 rows of one device, at most 6 routes name any one expert below 1; on every device of one index of dp, one same expert below 1 is named by exactly 6 routes.
All inputs are finite; a program needn't handle non-finite values.
Results may differ from a plain program's by a relative error of at most 0.02.
Values may be sent and summed in bfloat16 or wider, within the bound.
A program may use at most 128 MiB of HBM per device.

v0:
```python
import jax
import jax.numpy as jnp
from jax import lax
from jax.sharding import PartitionSpec as P

HSPLIT = 16
CAP = 6


def copies(values, experts):
    grouped = values.reshape((experts, CAP) + values.shape[1:])
    return jnp.repeat(grouped, HSPLIT, axis=0)


def forward_part(slot_tokens, gate_slab, up_slab):
    pre_gate = jnp.dot(slot_tokens, gate_slab, preferred_element_type=jnp.float32)
    pre_up = jnp.dot(slot_tokens, up_slab, preferred_element_type=jnp.float32)
    sigmoid_gate = jax.nn.sigmoid(pre_gate)
    activation = pre_gate * sigmoid_gate
    hidden = (activation * pre_up).astype(jnp.bfloat16)
    return (pre_gate, pre_up, sigmoid_gate, activation, hidden)


def shards(tokens, cotangent, route_ids, gates, w_gate, w_up, w_down):
    slabs = lax.axis_size("expert")
    experts = slabs // HSPLIT
    tok_count, features = tokens.shape
    top_count = route_ids.shape[1]
    slot_total = experts * CAP
    flat_ids = route_ids.reshape(-1)
    expert_hits = (flat_ids[:, None] == jnp.arange(experts, dtype=jnp.int32)[None, :]).astype(
        jnp.int32
    )
    earlier = jnp.cumsum(expert_hits, axis=0) - expert_hits
    slot_rank = jnp.sum(earlier * expert_hits, axis=1)
    in_slab = jnp.sum(expert_hits, axis=1) > 0
    slot_index = flat_ids * CAP + slot_rank
    table = (slot_index[:, None] == jnp.arange(slot_total, dtype=jnp.int32)[None, :]) & in_slab[
        :, None
    ]
    select = table.reshape(tok_count, top_count, slot_total)
    picked = jnp.any(select, axis=1)
    pick_half = picked.astype(jnp.bfloat16)
    token_slots = jnp.einsum(
        "tc,td->cd", pick_half, tokens, preferred_element_type=jnp.float32
    ).astype(jnp.bfloat16)
    cotan_slots = jnp.einsum(
        "tc,td->cd", pick_half, cotangent, preferred_element_type=jnp.float32
    ).astype(jnp.bfloat16)
    gate_slots = jnp.sum(
        jnp.where(select, gates[:, :, None].astype(jnp.float32), 0.0), axis=(0, 1)
    ).astype(jnp.bfloat16)
    send_tok = copies(token_slots, experts)
    send_cotan = copies(cotan_slots, experts)
    send_gate = copies(gate_slots, experts)
    new_gate, new_up, new_down = (
        lax.all_to_all(w_gate, "dp", split_axis=1, concat_axis=2, tiled=True),
        lax.all_to_all(w_up, "dp", split_axis=1, concat_axis=2, tiled=True),
        lax.all_to_all(w_down, "dp", split_axis=1, concat_axis=2, tiled=True),
    )
    full_gate, full_up, full_down = (
        lax.all_gather(new_gate, "dp", axis=1, tiled=True),
        lax.all_gather(new_up, "dp", axis=1, tiled=True),
        lax.all_gather(new_down, "dp", axis=1, tiled=True),
    )
    gate_slab = full_gate[0]
    up_slab = full_up[0]
    down_slab = full_down[0]
    recv_tok, recv_cotan, recv_gate = (
        lax.all_to_all(send_tok, "expert", split_axis=0, concat_axis=0, tiled=True),
        lax.all_to_all(send_cotan, "expert", split_axis=0, concat_axis=0, tiled=True),
        lax.all_to_all(send_gate, "expert", split_axis=0, concat_axis=0, tiled=True),
    )
    slot_tokens = recv_tok.reshape(-1, features)
    pre_gate, pre_up, sigmoid_gate, activation, hidden = forward_part(
        slot_tokens, gate_slab, up_slab
    )
    slot_cotan = recv_cotan.reshape(-1, features)
    slot_gates = recv_gate.reshape(-1).astype(jnp.float32)[:, None]
    back_proj = jnp.dot(slot_cotan, down_slab, preferred_element_type=jnp.float32)
    score_part = jnp.sum(hidden.astype(jnp.float32) * back_proj, axis=1).astype(jnp.bfloat16)
    scaled = slot_gates * back_proj
    d_gate = (scaled * pre_up * sigmoid_gate * (1.0 + pre_gate * (1.0 - sigmoid_gate))).astype(
        jnp.bfloat16
    )
    d_up = (scaled * activation).astype(jnp.bfloat16)
    hidden_gated = (slot_gates * hidden.astype(jnp.float32)).astype(jnp.bfloat16)
    partial_value = (
        jnp.einsum("rh,dh->rd", d_gate, gate_slab, preferred_element_type=jnp.float32)
        + jnp.einsum("rh,dh->rd", d_up, up_slab, preferred_element_type=jnp.float32)
    ).astype(jnp.bfloat16)
    grad_gate_part = jnp.einsum(
        "rd,rh->dh", slot_tokens, d_gate, preferred_element_type=jnp.float32
    )
    grad_up_part = jnp.einsum("rd,rh->dh", slot_tokens, d_up, preferred_element_type=jnp.float32)
    grad_down_part = jnp.einsum(
        "rd,rh->dh", slot_cotan, hidden_gated, preferred_element_type=jnp.float32
    )
    grad_gate, grad_up, grad_down = (
        lax.psum_scatter(
            grad_gate_part[None].astype(jnp.bfloat16), "dp", scatter_dimension=1, tiled=True
        ).astype(jnp.float32),
        lax.psum_scatter(
            grad_up_part[None].astype(jnp.bfloat16), "dp", scatter_dimension=1, tiled=True
        ).astype(jnp.float32),
        lax.psum_scatter(
            grad_down_part[None].astype(jnp.bfloat16), "dp", scatter_dimension=1, tiled=True
        ).astype(jnp.float32),
    )
    back_parts, back_scores = (
        lax.all_to_all(
            partial_value.reshape(slabs, CAP, features),
            "expert",
            split_axis=0,
            concat_axis=0,
            tiled=True,
        ),
        lax.all_to_all(
            score_part.reshape(slabs, CAP), "expert", split_axis=0, concat_axis=0, tiled=True
        ),
    )
    part_sum = jnp.sum(
        back_parts.reshape(experts, HSPLIT, CAP, features).astype(jnp.float32), axis=1
    )
    part_sum = part_sum.reshape(slot_total, features)
    score_sum = jnp.sum(
        back_scores.reshape(experts, HSPLIT, CAP).astype(jnp.float32), axis=1
    ).reshape(slot_total)
    token_grad = jnp.einsum(
        "tc,cd->td", picked.astype(jnp.float32), part_sum, precision=lax.Precision.HIGHEST
    ).astype(jnp.bfloat16)
    gate_grad = jnp.einsum(
        "tkc,c->tk", select.astype(jnp.float32), score_sum, precision=lax.Precision.HIGHEST
    )
    return (new_gate, new_up, new_down, grad_gate, grad_up, grad_down, token_grad, gate_grad)


def solution(mesh):
    in_specs = (
        P(("dp", "expert"), None),
        P(("dp", "expert"), None),
        P(("dp", "expert"), None),
        P(("dp", "expert"), None),
        P("expert", None, "dp"),
        P("expert", None, "dp"),
        P("expert", None, "dp"),
    )
    out_specs = (
        P("expert", "dp", None),
        P("expert", "dp", None),
        P("expert", "dp", None),
        P("expert", "dp", None),
        P("expert", "dp", None),
        P("expert", "dp", None),
        P(("dp", "expert"), None),
        P(("dp", "expert"), None),
    )
    return jax.shard_map(shards, mesh=mesh, in_specs=in_specs, out_specs=out_specs, check_vma=False)
```

profile of v0, /device:TPU:0, one launch (start us, length us, event | category | flops | bytes accessed | tf_op | source)
XLA Modules:
  0.0 288.6 jit_solution(10073524638318740197)
XLA Ops:
  7.2 0.8 fusion.21
  8.1 0.3 reduce-window.6
  8.7 0.7 convert_element_type.136
  9.9 0.7 select_add_fusion
  10.7 0.6 reshape.208
  11.3 7.4 %all-to-all-start.4 = ((bf16[16,1,6]{2,1,0:T(2,128)(2,1)}), bf16[16,1,6]{2,1,0:T(2,128)(2,1)S(1)}, u32[]{:S(2)}, u32[]{:S(2)}) async-start(bf16[16,1,6]{2,1,0:T(2,128)(2,1)} %reshape.208), calls=%async_computation.4 | async-start | bytes 16384 | tf_op jit(solution)/shard_map/all_to_all | solution.py:72
  18.7 4.2 %copy.84 = bf16[1,3584,64]{2,0,1:T(2,128)(2,1)S(1)} copy(bf16[1,3584,64]{1,2,0:T(8,128)(2,1)} %param.11) | data formatting | bytes 917504 | tf_op args[4]
  22.9 0.5 broadcast.89
  23.4 20.6 %reduce.10 = bf16[3584,64]{1,0:T(8,128)(2,1)} reduce(bf16[3584,1,64]{2,1,0:T(2,128)(2,1)S(1)} %bitcast.66, bf16[]{:T(256)} %broadcast.89), dimensions={1}, to_apply=%bitcast.42.reduce_sub_computation | reduce | bytes 917506
  44.0 2.5 reshape.224
  46.5 3.5 %all-to-all-start = ((bf16[2,2,57344]{2,1,0:T(2,128)(2,1)}), bf16[2,2,57344]{2,1,0:T(2,128)(2,1)S(1)}, u32[]{:S(2)}, u32[]{:S(2)}) async-start(bf16[2,2,57344]{2,1,0:T(2,128)(2,1)} %reshape.224), calls=%async_computation | async-start | bytes 917504 | tf_op jit(solution)/shard_map/all_to_all | solution.py:57
  50.0 4.2 %copy.87 = bf16[1,3584,64]{2,0,1:T(2,128)(2,1)S(1)} copy(bf16[1,3584,64]{1,2,0:T(8,128)(2,1)} %param.12) | data formatting | bytes 917504 | tf_op args[5]
  54.2 20.6 %reduce.11 = bf16[3584,64]{1,0:T(8,128)(2,1)} reduce(bf16[3584,1,64]{2,1,0:T(2,128)(2,1)S(1)} %bitcast.71, bf16[]{:T(256)} %broadcast.89), dimensions={1}, to_apply=%bitcast.44.reduce_sub_computation | reduce | bytes 917506
  74.8 2.5 reshape.226
  77.2 4.4 %all-to-all-start.1 = ((bf16[2,2,57344]{2,1,0:T(2,128)(2,1)}), bf16[2,2,57344]{2,1,0:T(2,128)(2,1)}, u32[]{:S(2)}, u32[]{:S(2)}) async-start(bf16[2,2,57344]{2,1,0:T(2,128)(2,1)} %reshape.226), calls=%async_computation.1 | async-start | bytes 917504 | tf_op jit(solution)/shard_map/all_to_all | solution.py:58
  81.6 4.2 %copy.90 = bf16[1,3584,64]{2,0,1:T(2,128)(2,1)S(1)} copy(bf16[1,3584,64]{1,2,0:T(8,128)(2,1)} %param.13) | data formatting | bytes 917504 | tf_op args[6]
  85.8 20.6 %reduce.12 = bf16[3584,64]{1,0:T(8,128)(2,1)} reduce(bf16[3584,1,64]{2,1,0:T(2,128)(2,1)S(1)} %bitcast.67, bf16[]{:T(256)} %broadcast.89), dimensions={1}, to_apply=%bitcast.46.reduce_sub_computation | reduce | bytes 917506
  106.4 2.5 reshape.228
  108.9 3.5 %all-to-all-start.2 = ((bf16[2,2,57344]{2,1,0:T(2,128)(2,1)}), bf16[2,2,57344]{2,1,0:T(2,128)(2,1)S(1)}, u32[]{:S(2)}, u32[]{:S(2)}) async-start(bf16[2,2,57344]{2,1,0:T(2,128)(2,1)} %reshape.228), calls=%async_computation.2 | async-start | bytes 917504 | tf_op jit(solution)/shard_map/all_to_all | solution.py:59
  112.7 7.9 %all-to-all-done.2 = bf16[2,2,57344]{2,1,0:T(2,128)(2,1)S(1)} async-done(((bf16[2,2,57344]{2,1,0:T(2,128)(2,1)}), bf16[2,2,57344]{2,1,0:T(2,128)(2,1)S(1)}, u32[]{:S(2)}, u32[]{:S(2)}) %all-to-all-start.2) | async-done | bytes 458784 | tf_op jit(solution)/shard_map/all_to_all | solution.py:59
  120.6 1.1 reshape.206
  121.6 5.7 %all-to-all-start.3 = ((bf16[16,6,3584]{2,1,0:T(8,128)(2,1)}), bf16[16,6,3584]{2,1,0:T(8,128)(2,1)S(1)}, u32[]{:S(2)}, u32[]{:S(2)}) async-start(bf16[16,6,3584]{2,1,0:T(8,128)(2,1)} %reshape.206), calls=%async_computation.3 | async-start | bytes 1835008 | tf_op jit(solution)/shard_map/all_to_all | solution.py:70
  127.6 20.6 %all-to-all-done.3 = bf16[16,6,3584]{2,1,0:T(8,128)(2,1)S(1)} async-done(((bf16[16,6,3584]{2,1,0:T(8,128)(2,1)}), bf16[16,6,3584]{2,1,0:T(8,128)(2,1)S(1)}, u32[]{:S(2)}, u32[]{:S(2)}) %all-to-all-start.3) | async-done | bytes 688160 | tf_op jit(solution)/shard_map/all_to_all | solution.py:70
  148.2 1.1 reshape.209
  149.3 6.2 %all-to-all-start.5 = ((bf16[16,6,3584]{2,1,0:T(8,128)(2,1)}), bf16[16,6,3584]{2,1,0:T(8,128)(2,1)}, u32[]{:S(2)}, u32[]{:S(2)}) async-start(bf16[16,6,3584]{2,1,0:T(8,128)(2,1)} %reshape.209), calls=%async_computation.5 | async-start | bytes 1835008 | tf_op jit(solution)/shard_map/all_to_all | solution.py:71
  155.7 0.7 reshape.225
  156.4 2.1 copy.85
  158.6 1.8 reshape.227
  160.4 3.1 %copy.88 = bf16[1,3584,64]{1,2,0:T(8,128)(2,1)} copy(bf16[1,3584,64]{2,0,1:T(2,128)(2,1)S(1)} %bitcast.69) | data formatting | bytes 917504 | tf_op jit(solution)/shard_map/all_to_all | solution.py:58
  163.5 1.1 all_to_all.61
  164.6 0.8 copy.89
  165.5 1.6 reshape.229
  167.1 3.1 %copy.91 = bf16[1,3584,64]{1,2,0:T(8,128)(2,1)} copy(bf16[1,3584,64]{2,0,1:T(2,128)(2,1)S(1)} %bitcast.70) | data formatting | bytes 917504 | tf_op jit(solution)/shard_map/all_to_all | solution.py:59
  170.2 1.1 all_to_all.65
  171.4 13.6 %all_gather.11 = bf16[1,3584,128]{1,2,0:T(8,128)(2,1)S(1)} all-gather(bf16[1,1792,128]{1,2,0:T(8,128)(2,1)S(1)} %bitcast.72), channel_id=1, replica_groups=mesh['dp'=2,'expert'=16] {'dp'}, dimensions={1}, use_global_device_ids=true | all-gather | bytes 1376256 | tf_op jit(solution)/shard_map/all_gather | solution.py:62
  185.0 12.6 %all_gather.10 = bf16[1,3584,128]{1,2,0:T(8,128)(2,1)S(1)} all-gather(bf16[1,1792,128]{1,2,0:T(8,128)(2,1)S(1)} %bitcast.74), channel_id=1, replica_groups=mesh['dp'=2,'expert'=16] {'dp'}, dimensions={1}, use_global_device_ids=true | all-gather | bytes 1376256 | tf_op jit(solution)/shard_map/all_gather | solution.py:63
  197.7 11.8 %all_gather.9 = bf16[1,3584,128]{1,2,0:T(8,128)(2,1)} all-gather(bf16[1,1792,128]{1,2,0:T(8,128)(2,1)S(1)} %bitcast.76), channel_id=1, replica_groups=mesh['dp'=2,'expert'=16] {'dp'}, dimensions={1}, use_global_device_ids=true | all-gather | bytes 1376256 | tf_op jit(solution)/shard_map/all_gather | solution.py:64
  209.5 1.4 reshape.207
  210.9 0.4 fusion.6
  211.3 1.1 fusion.9
  212.4 2.1 reshape.210
  214.5 2.5 fusion.14
  217.0 1.4 fusion.3
  218.4 1.4 fusion.1
  219.8 0.7 convert_element_type.163
  220.6 5.3 %all-to-all-start.7 = ((bf16[16,1,6]{2,1,0:T(2,128)(2,1)}), bf16[16,1,6]{2,1,0:T(2,128)(2,1)S(1)}, u32[]{:S(2)}, u32[]{:S(2)}) async-start(bf16[16,1,6]{2,1,0:T(2,128)(2,1)} %convert_element_type.163), calls=%async_computation.10 | async-start | bytes 16384 | tf_op jit(solution)/shard_map/all_to_all | solution.py:118
  225.8 0.3 reduce-scatter.6.cloned.1.call-start
  226.1 1.4 fusion.2
  227.5 1.4 fusion.4
  228.9 1.7 fusion
  230.7 1.2 reshape.211
  231.8 0.4 all-to-all-done.7
  232.2 5.8 %all-to-all-start.6 = ((bf16[16,6,3584]{2,1,0:T(8,128)(2,1)}), bf16[16,6,3584]{2,1,0:T(8,128)(2,1)}, u32[]{:S(2)}, u32[]{:S(2)}) async-start(bf16[16,6,3584]{2,1,0:T(8,128)(2,1)} %reshape.211), calls=%async_computation.9 | async-start | bytes 1835008 | tf_op jit(solution)/shard_map/all_to_all | solution.py:111
  238.0 1.0 copy.97
  239.0 1.0 copy.98
  240.0 1.0 copy.99
  241.0 0.7 fusion.19
  241.7 17.2 %all-to-all-done.6 = bf16[16,6,3584]{2,1,0:T(8,128)(2,1)} async-done(((bf16[16,6,3584]{2,1,0:T(8,128)(2,1)}), bf16[16,6,3584]{2,1,0:T(8,128)(2,1)}, u32[]{:S(2)}, u32[]{:S(2)}) %all-to-all-start.6) | async-done | bytes 688160 | tf_op jit(solution)/shard_map/all_to_all | solution.py:111
  258.9 1.4 convert_reduce_fusion
  260.3 1.9 convolution_convert_fusion
  262.1 2.0 convert_element_type.154
  264.1 2.0 convert_element_type.144
  266.1 13.9 %reduce-scatter.6.cloned.1.call-done = bf16[1,1792,128]{2,1,0:T(8,128)(2,1)} async-done(((bf16[1,3584,128]{2,1,0:T(8,128)(2,1)}), bf16[1,1792,128]{2,1,0:T(8,128)(2,1)}) %reduce-scatter.6.cloned.1.call-update) | async-done | bytes 458768 | tf_op jit(solution)/shard_map/reduce_scatter | solution.py:103
  280.1 2.0 convert_element_type.148
  (55 shorter events, 2.1 us)
Async XLA Ops:
  7.2 105.3 %copy-start = (bf16[128,3584]{1,0:T(8,128)(2,1)S(1)}, bf16[128,3584]{1,0:T(8,128)(2,1)}, u32[]{:S(2)}) copy-start(bf16[128,3584]{1,0:T(8,128)(2,1)} %param.7) | copy-start | bytes 2752516
  11.3 35.2 %all-to-all-start.4 = ((bf16[16,1,6]{2,1,0:T(2,128)(2,1)}), bf16[16,1,6]{2,1,0:T(2,128)(2,1)S(1)}, u32[]{:S(2)}, u32[]{:S(2)}) async-start(bf16[16,1,6]{2,1,0:T(2,128)(2,1)} %reshape.208), calls=%async_computation.4 | async-start | bytes 16384 | tf_op jit(solution)/shard_map/all_to_all | solution.py:72
  46.5 30.8 %all-to-all-start = ((bf16[2,2,57344]{2,1,0:T(2,128)(2,1)}), bf16[2,2,57344]{2,1,0:T(2,128)(2,1)S(1)}, u32[]{:S(2)}, u32[]{:S(2)}) async-start(bf16[2,2,57344]{2,1,0:T(2,128)(2,1)} %reshape.224), calls=%async_computation | async-start | bytes 917504 | tf_op jit(solution)/shard_map/all_to_all | solution.py:57
  77.2 31.7 %all-to-all-start.1 = ((bf16[2,2,57344]{2,1,0:T(2,128)(2,1)}), bf16[2,2,57344]{2,1,0:T(2,128)(2,1)}, u32[]{:S(2)}, u32[]{:S(2)}) async-start(bf16[2,2,57344]{2,1,0:T(2,128)(2,1)} %reshape.226), calls=%async_computation.1 | async-start | bytes 917504 | tf_op jit(solution)/shard_map/all_to_all | solution.py:58
  108.9 11.6 %all-to-all-start.2 = ((bf16[2,2,57344]{2,1,0:T(2,128)(2,1)}), bf16[2,2,57344]{2,1,0:T(2,128)(2,1)S(1)}, u32[]{:S(2)}, u32[]{:S(2)}) async-start(bf16[2,2,57344]{2,1,0:T(2,128)(2,1)} %reshape.228), calls=%async_computation.2 | async-start | bytes 917504 | tf_op jit(solution)/shard_map/all_to_all | solution.py:59
  112.4 14.9 %copy-start.10 = (bf16[128,3584]{1,0:T(8,128)(2,1)S(1)}, bf16[128,3584]{1,0:T(8,128)(2,1)}, u32[]{:S(2)}) copy-start(bf16[128,3584]{1,0:T(8,128)(2,1)} %param.8) | copy-start | bytes 2752516
  120.6 1.1 copy-start.9
  121.6 26.5 %all-to-all-start.3 = ((bf16[16,6,3584]{2,1,0:T(8,128)(2,1)}), bf16[16,6,3584]{2,1,0:T(8,128)(2,1)S(1)}, u32[]{:S(2)}, u32[]{:S(2)}) async-start(bf16[16,6,3584]{2,1,0:T(8,128)(2,1)} %reshape.206), calls=%async_computation.3 | async-start | bytes 1835008 | tf_op jit(solution)/shard_map/all_to_all | solution.py:70
  148.2 7.4 %copy-start.8 = (bf16[16,6,3584]{2,1,0:T(8,128)(2,1)}, bf16[16,6,3584]{2,1,0:T(8,128)(2,1)S(1)}, u32[]{:S(2)}) copy-start(bf16[16,6,3584]{2,1,0:T(8,128)(2,1)S(1)} %all-to-all-done.3) | copy-start | bytes 2064388
  149.3 63.1 %all-to-all-start.5 = ((bf16[16,6,3584]{2,1,0:T(8,128)(2,1)}), bf16[16,6,3584]{2,1,0:T(8,128)(2,1)}, u32[]{:S(2)}, u32[]{:S(2)}) async-start(bf16[16,6,3584]{2,1,0:T(8,128)(2,1)} %reshape.209), calls=%async_computation.5 | async-start | bytes 1835008 | tf_op jit(solution)/shard_map/all_to_all | solution.py:71
  155.5 106.6 %reduce-scatter.8.cloned.1.call-start = ((), (), s32[]{:S(2)}) async-start(), calls=%async_computation.13 | async-start | bytes 1376256 | tf_op jit(solution)/shard_map/reduce_scatter | solution.py:106
  158.6 12.8 %copy-start.2 = (bf16[1,1792,2,64]{1,3,2,0:T(8,128)(2,1)}, bf16[1,1792,2,64]{1,3,2,0:T(8,128)(2,1)S(1)}, u32[]{:S(2)}) copy-start(bf16[1,1792,2,64]{1,3,2,0:T(8,128)(2,1)S(1)} %copy.86) | copy-start | bytes 1376260
  171.3 13.7 %copy-start.4 = (bf16[1,1792,2,64]{1,3,2,0:T(8,128)(2,1)S(1)}, bf16[1,1792,2,64]{1,3,2,0:T(8,128)(2,1)}, u32[]{:S(2)}) copy-start(bf16[1,1792,2,64]{1,3,2,0:T(8,128)(2,1)} %copy.89) | copy-start | bytes 1376260
  171.4 26.3 %copy-start.6 = (bf16[1,1792,2,64]{1,3,2,0:T(8,128)(2,1)}, bf16[1,1792,2,64]{1,3,2,0:T(8,128)(2,1)S(1)}, u32[]{:S(2)}) copy-start(bf16[1,1792,2,64]{1,3,2,0:T(8,128)(2,1)S(1)} %copy.92) | copy-start | bytes 1376260
  214.5 2.5 copy-start.1
  218.4 1.5 copy-start.11
  218.4 45.7 %reduce-scatter.4.cloned.1.call-start = ((), (), s32[]{:S(2)}) async-start(), calls=%async_computation.11 | async-start | bytes 1376256 | tf_op jit(solution)/shard_map/reduce_scatter | solution.py:100
  220.6 11.6 %all-to-all-start.7 = ((bf16[16,1,6]{2,1,0:T(2,128)(2,1)}), bf16[16,1,6]{2,1,0:T(2,128)(2,1)S(1)}, u32[]{:S(2)}, u32[]{:S(2)}) async-start(bf16[16,1,6]{2,1,0:T(2,128)(2,1)} %convert_element_type.163), calls=%async_computation.10 | async-start | bytes 16384 | tf_op jit(solution)/shard_map/all_to_all | solution.py:118
  225.8 54.2 %reduce-scatter.6.cloned.1.call-start = ((), (), s32[]{:S(2)}) async-start(), calls=%async_computation.12 | async-start | bytes 1376256 | tf_op jit(solution)/shard_map/reduce_scatter | solution.py:103
  230.6 7.4 %copy-start.3 = (bf16[1,1792,2,64]{1,3,2,0:T(8,128)(2,1)S(1)}, bf16[1,1792,2,64]{1,3,2,0:T(8,128)(2,1)}, u32[]{:S(2)}) copy-start(bf16[1,1792,2,64]{1,3,2,0:T(8,128)(2,1)} %copy-done.2) | copy-start | bytes 1376260
  230.6 8.4 %copy-start.5 = (bf16[1,1792,2,64]{1,3,2,0:T(8,128)(2,1)S(1)}, bf16[1,1792,2,64]{1,3,2,0:T(8,128)(2,1)}, u32[]{:S(2)}) copy-start(bf16[1,1792,2,64]{1,3,2,0:T(8,128)(2,1)} %copy.89) | copy-start | bytes 1376260
  231.8 8.2 %copy-start.7 = (bf16[1,1792,2,64]{1,3,2,0:T(8,128)(2,1)S(1)}, bf16[1,1792,2,64]{1,3,2,0:T(8,128)(2,1)}, u32[]{:S(2)}) copy-start(bf16[1,1792,2,64]{1,3,2,0:T(8,128)(2,1)} %copy-done.6) | copy-start | bytes 1376260
  232.2 26.7 %all-to-all-start.6 = ((bf16[16,6,3584]{2,1,0:T(8,128)(2,1)}), bf16[16,6,3584]{2,1,0:T(8,128)(2,1)}, u32[]{:S(2)}, u32[]{:S(2)}) async-start(bf16[16,6,3584]{2,1,0:T(8,128)(2,1)} %reshape.211), calls=%async_computation.9 | async-start | bytes 1835008 | tf_op jit(solution)/shard_map/all_to_all | solution.py:111
Sparse Core Ops, SparseCore 0:
  218.5 18.5 reduce-scatter.7
  240.0 18.8 reduce-scatter.3
  261.2 18.8 reduce-scatter.5
where the time goes:
time: 290 us; the launch traced here: 289 us
  other arithmetic  72.1 us (25%)
  waiting for transfers between devices  60 us (21%)
  local copies, waits for them, and re-layouts  48 us (17%)
  starting transfers between devices  42.1 us (15%)
  blocking collectives  38.1 us (13%)
  matrix products  14.2 us (5%)
  between operations  14.1 us (5%)
    unnamed x3, other arithmetic  61.8 us
    unnamed x37, local copies, waits for them, and re-layouts  27.6 us
    all_to_all x1, waiting for transfers between devices, shards(): lax.all_to_all(send_tok, 'expert', split_axis=0, concat_axis=0, tiled=True)  20.6 us
    all_to_all x1, waiting for transfers between devices, shards(): lax.all_to_all(partial_value.reshape(slabs, CAP, features), 'expert', spl...  17.2 us
    reduce_scatter x1, waiting for transfers between devices, shards(): lax.psum_scatter(grad_up_part[None].astype(jnp.bfloat16), 'dp', scatter_d...  13.9 us
    all_gather x1, blocking collectives, shards(): lax.all_gather(new_gate, 'dp', axis=1, tiled=True)  13.6 us
    all_gather x1, blocking collectives, shards(): lax.all_gather(new_up, 'dp', axis=1, tiled=True)  12.6 us
    all_gather x1, blocking collectives, shards(): lax.all_gather(new_down, 'dp', axis=1, tiled=True)  11.8 us
  transfers between devices with their start and end apart: 11, of which 5 were waited for; matrix products, arithmetic and copies ran while one was open for 41% of the time, Pallas kernels for 0%

commit v1 on v0

v1 whole, which is shorter than its diff:
```python
import jax
import jax.numpy as jnp
from jax import lax
from jax.sharding import PartitionSpec as P

HSPLIT = 16
CAP = 6


def shards(tokens, cotangent, route_ids, gates, w_gate, w_up, w_down):
    slabs = lax.axis_size("expert")
    groups = lax.axis_size("dp")
    experts = slabs // HSPLIT
    tok_count, features = tokens.shape
    part = features // groups
    top_count = route_ids.shape[1]
    slot_total = experts * CAP
    flat_ids = route_ids.reshape(-1)
    expert_hits = (flat_ids[:, None] == jnp.arange(experts, dtype=jnp.int32)[None, :]).astype(
        jnp.int32
    )
    earlier = jnp.cumsum(expert_hits, axis=0) - expert_hits
    slot_rank = jnp.sum(earlier * expert_hits, axis=1)
    in_slab = jnp.sum(expert_hits, axis=1) > 0
    slot_index = flat_ids * CAP + slot_rank
    table = (slot_index[:, None] == jnp.arange(slot_total, dtype=jnp.int32)[None, :]) & in_slab[
        :, None
    ]
    select = table.reshape(tok_count, top_count, slot_total)
    picked = jnp.any(select, axis=1)
    pick_half = picked.astype(jnp.bfloat16)
    token_slots = jnp.einsum(
        "tc,td->cd", pick_half, tokens, preferred_element_type=jnp.float32
    ).astype(jnp.bfloat16)
    cotan_slots = jnp.einsum(
        "tc,td->cd", pick_half, cotangent, preferred_element_type=jnp.float32
    ).astype(jnp.bfloat16)
    gate_slots = jnp.sum(
        jnp.where(select, gates[:, :, None].astype(jnp.float32), 0.0), axis=(0, 1)
    ).astype(jnp.bfloat16)
    weights = jnp.stack([w_gate[0], w_up[0], w_down[0]])
    relaid = lax.all_to_all(weights, "dp", split_axis=1, concat_axis=2, tiled=True)
    both = jnp.stack([token_slots, cotan_slots]).reshape(2, experts, CAP, groups, part)
    both = jnp.moveaxis(both, 3, 0)
    both = lax.all_to_all(both, "dp", split_axis=0, concat_axis=0, tiled=True)
    gate_all = lax.all_gather(gate_slots.reshape(experts, CAP), "dp", axis=0, tiled=False)
    if experts == 1:
        recv = lax.all_gather(both, "expert", axis=0, tiled=False)[:, :, :, 0]
        gate_recv = lax.all_gather(gate_all, "expert", axis=0, tiled=False)[:, :, 0]
    else:
        send = jnp.repeat(jnp.moveaxis(both, 2, 0), HSPLIT, axis=0)
        recv = lax.all_to_all(send, "expert", split_axis=0, concat_axis=0, tiled=True)
        gate_send = jnp.repeat(jnp.moveaxis(gate_all, 1, 0), HSPLIT, axis=0)
        gate_recv = lax.all_to_all(gate_send, "expert", split_axis=0, concat_axis=0, tiled=True)
    slot_tokens = recv[:, :, 0].reshape(-1, part)
    slot_cotan = recv[:, :, 1].reshape(-1, part)
    slot_gates = gate_recv.reshape(-1).astype(jnp.float32)[:, None]
    pre_part = jnp.stack(
        [
            jnp.dot(slot_tokens, relaid[0], preferred_element_type=jnp.float32),
            jnp.dot(slot_tokens, relaid[1], preferred_element_type=jnp.float32),
            jnp.dot(slot_cotan, relaid[2], preferred_element_type=jnp.float32),
        ]
    )
    pre_gate, pre_up, back_proj = lax.psum(pre_part, "dp")
    sigmoid_gate = jax.nn.sigmoid(pre_gate)
    activation = pre_gate * sigmoid_gate
    hidden = (activation * pre_up).astype(jnp.bfloat16)
    score_part = jnp.sum(hidden.astype(jnp.float32) * back_proj, axis=1).astype(jnp.bfloat16)
    scaled = slot_gates * back_proj
    d_gate = (scaled * pre_up * sigmoid_gate * (1.0 + pre_gate * (1.0 - sigmoid_gate))).astype(
        jnp.bfloat16
    )
    d_up = (scaled * activation).astype(jnp.bfloat16)
    hidden_gated = (slot_gates * hidden.astype(jnp.float32)).astype(jnp.bfloat16)
    partial_value = (
        jnp.einsum("rh,dh->rd", d_gate, relaid[0], preferred_element_type=jnp.float32)
        + jnp.einsum("rh,dh->rd", d_up, relaid[1], preferred_element_type=jnp.float32)
    ).astype(jnp.bfloat16)
    grad_gate = jnp.einsum("rd,rh->dh", slot_tokens, d_gate, preferred_element_type=jnp.float32)
    grad_up = jnp.einsum("rd,rh->dh", slot_tokens, d_up, preferred_element_type=jnp.float32)
    grad_down = jnp.einsum(
        "rd,rh->dh", slot_cotan, hidden_gated, preferred_element_type=jnp.float32
    )
    rows = groups * CAP
    back_parts = lax.all_to_all(
        partial_value.reshape(slabs, rows, part), "expert", split_axis=0, concat_axis=0, tiled=True
    )
    back_scores = lax.all_to_all(
        score_part.reshape(slabs, rows), "expert", split_axis=0, concat_axis=0, tiled=True
    )
    part_sum = jnp.sum(
        back_parts.reshape(experts, HSPLIT, groups, CAP, part).astype(jnp.float32), axis=1
    ).astype(jnp.bfloat16)
    part_sum = lax.all_to_all(
        jnp.moveaxis(part_sum, 1, 0), "dp", split_axis=0, concat_axis=3, tiled=True
    ).reshape(slot_total, features)
    own = lax.axis_index("dp")
    score_sum = jnp.sum(
        back_scores.reshape(experts, HSPLIT, groups, CAP).astype(jnp.float32), axis=1
    )
    score_sum = lax.dynamic_index_in_dim(score_sum, own, 1, keepdims=False).reshape(slot_total)
    token_grad = jnp.einsum(
        "tc,cd->td", pick_half, part_sum, preferred_element_type=jnp.float32
    ).astype(jnp.bfloat16)
    gate_grad = jnp.einsum(
        "tkc,c->tk", select.astype(jnp.float32), score_sum, precision=lax.Precision.HIGHEST
    )
    return (
        relaid[0:1],
        relaid[1:2],
        relaid[2:3],
        grad_gate[None],
        grad_up[None],
        grad_down[None],
        token_grad,
        gate_grad,
    )


def solution(mesh):
    in_specs = (
        P(("dp", "expert"), None),
        P(("dp", "expert"), None),
        P(("dp", "expert"), None),
        P(("dp", "expert"), None),
        P("expert", None, "dp"),
        P("expert", None, "dp"),
        P("expert", None, "dp"),
    )
    out_specs = (
        P("expert", "dp", None),
        P("expert", "dp", None),
        P("expert", "dp", None),
        P("expert", "dp", None),
        P("expert", "dp", None),
        P("expert", "dp", None),
        P(("dp", "expert"), None),
        P(("dp", "expert"), None),
    )
    return jax.shard_map(shards, mesh=mesh, in_specs=in_specs, out_specs=out_specs, check_vma=False)
```

time: 290 us -> 165 us (0.57)
  other arithmetic: 72.1 us -> 10.1 us
  waiting for transfers between devices: 60 us -> 15.5 us
  starting transfers between devices: 42.1 us -> 12 us
  blocking collectives: 38.1 us -> 54.8 us
  local copies, waits for them, and re-layouts: 48 us -> 43.8 us
    unnamed x3 -> x0, other arithmetic: 61.8 us -> none
    all_to_all x8 -> x3, waiting for transfers between devices: 46 us -> 15.5 us  [the longest x1 10.6 us: shards(): lax.all_to_all(partial_value.reshape(slabs, rows, part), 'expert', split_...]
    all_to_all x8 -> x3, starting transfers between devices: 41.7 us -> 11.9 us  [the longest x1 4.53 us: shards(): lax.all_to_all(partial_value.reshape(slabs, rows, part), 'expert', split_...]
    all_to_all x0 -> x2, blocking collectives: none -> 28 us  [the longest x1 19.7 us: shards(): lax.all_to_all(weights, 'dp', split_axis=1, concat_axis=2, tiled=True)]
    all_gather x3 -> x1, blocking collectives: 38.1 us -> 21.8 us  [shards(): gate_recv = lax.all_gather(gate_all, 'expert', axis=0, tiled=False)[:, :, 0]]
    unnamed x37 -> x36, local copies, waits for them, and re-layouts: 27.6 us -> 13.4 us
    reduce_scatter x3 -> x0, waiting for transfers between devices: 13.9 us -> none  [the longest x1 13.9 us: shards(): lax.psum_scatter(grad_up_part[None].astype(jnp.bfloat16), 'dp', scatter_d...]
    slice x1 -> x6, local copies, waits for them, and re-layouts: 0.19 us -> 10.7 us  [the longest x1 8.67 us: shards(): slot_cotan = recv[:, :, 1].reshape(-1, part)]
  transfers between devices with their start and end apart: 11 -> 5, of which waited for: 5 -> 3; matrix products, arithmetic and copies ran while one was open for 41% -> 25% of each run, Pallas kernels for 0% -> 0%
where the time goes in v1:
time: 165 us; the launch traced here: 164 us
  blocking collectives  54.8 us (33%)
  local copies, waits for them, and re-layouts  43.8 us (27%)
  waiting for transfers between devices  15.5 us (9%)
  between operations  15 us (9%)
  matrix products  12.7 us (8%)
  starting transfers between devices  12 us (7%)
  other arithmetic  10.1 us (6%)
    all_gather x1, blocking collectives, shards(): gate_recv = lax.all_gather(gate_all, 'expert', axis=0, tiled=False)[:, :, 0]  21.8 us
    all_to_all x1, blocking collectives, shards(): lax.all_to_all(weights, 'dp', split_axis=1, concat_axis=2, tiled=True)  19.7 us
    unnamed x36, local copies, waits for them, and re-layouts  13.4 us
    all_to_all x1, waiting for transfers between devices, shards(): lax.all_to_all(partial_value.reshape(slabs, rows, part), 'expert', split_...  10.6 us
    slice x1, local copies, waits for them, and re-layouts, shards(): slot_cotan = recv[:, :, 1].reshape(-1, part)  8.67 us
    all_to_all x1, local copies, waits for them, and re-layouts, shards(): lax.all_to_all(weights, 'dp', split_axis=1, concat_axis=2, tiled=True)  8.53 us
    all_to_all x1, blocking collectives, shards(): both = lax.all_to_all(both, 'dp', split_axis=0, concat_axis=0, tiled=True)  8.37 us
    unnamed x1, blocking collectives  4.92 us
  transfers between devices with their start and end apart: 5, of which 3 were waited for; matrix products, arithmetic and copies ran while one was open for 25% of the time, Pallas kernels for 0%

profile of v1, /device:TPU:0, one launch (start us, length us, event | category | flops | bytes accessed | tf_op | source)
XLA Modules:
  0.0 163.9 jit_solution(10995977781976014022)
XLA Ops:
  7.2 0.8 convert_compare_fusion
  8.1 0.1 copy.149
  8.2 0.1 reshape.250
  8.2 0.3 reduce-window.6
  8.5 0.2 slice_reduce_fusion.2
  8.7 0.1 reshape.243
  8.8 0.2 reduce-window.9
  9.0 0.1 broadcast.115
  9.1 0.1 reshape.246
  9.2 0.1 copy.150
  9.3 0.7 select_add_fusion
  10.1 0.2 convolution_convert_fusion.2
  10.3 0.1 copy.152
  10.4 0.2 convolution_convert_fusion.1
  10.7 0.1 copy.153
  10.8 0.2 maximum_bitcast_fusion
  11.0 8.4 %all_to_all.46 = bf16[2,2,1,6,1792]{4,1,3,2,0:T(2,128)(2,1)} all-to-all(bf16[2,2,1,6,1792]{4,1,3,2,0:T(2,128)(2,1)S(1)} %maximum_bitcast_fusion), channel_id=1, replica_groups=mesh['dp'=2,'expert'=16] {'dp'}, dimensions={0} | all-to-all | bytes 172032 | tf_op jit(solution)/shard_map/all_to_all | solution.py:45
  19.4 1.2 pad_maximum_fusion
  20.6 3.9 %copy.144 = bf16[3,3584,64]{2,0,1:T(4,128)(2,1)} copy(bf16[3,3584,64]{1,2,0:T(8,128)(2,1)S(1)} %pad_maximum_fusion) | data formatting | bytes 2752512 | tf_op jit(solution)/shard_map/stack | solution.py:41
  24.5 3.9 %reshape.277 = bf16[2,2,172032]{2,1,0:T(2,128)(2,1)S(1)} reshape(bf16[3584,3,64]{2,1,0:T(4,128)(2,1)} %bitcast.101) | data formatting | bytes 2752512
  28.5 19.7 %all_to_all.47 = bf16[2,2,172032]{2,1,0:T(2,128)(2,1)} all-to-all(bf16[2,2,172032]{2,1,0:T(2,128)(2,1)S(1)} %reshape.277), channel_id=1, replica_groups=mesh['dp'=2,'expert'=16] {'dp'}, dimensions={0} | all-to-all | bytes 2752512 | tf_op jit(solution)/shard_map/all_to_all | solution.py:42
  48.2 4.6 %reshape.278 = bf16[3584,3,64]{2,1,0:T(4,128)(2,1)} reshape(bf16[2,2,172032]{2,1,0:T(2,128)(2,1)} %all_to_all.47) | data formatting | bytes 2752512
  52.7 8.5 %copy.167 = bf16[3,2,1792,64]{2,1,3,0:T(2,128)(2,1)S(1)} copy(bf16[3,2,1792,64]{3,0,2,1:T(4,128)(2,1)} %bitcast.102) | data formatting | bytes 2752512 | tf_op jit(solution)/shard_map/all_to_all | solution.py:42
  61.3 0.9 fusion.25
  62.4 0.8 copy.148
  63.2 8.7 %slice_reduce_fusion = (bf16[16,2,6,1792]{3,2,1,0:T(8,128)(2,1)}, bf16[16,2,6,1792]{3,2,1,0:T(8,128)(2,1)S(1)}) fusion(bf16[16,2,2,6,1792]{4,2,3,1,0:T(2,128)(2,1)} %bitcast.110), kind=kLoop, calls=%fused_computation.8 | loop fusion | bytes 2752512 | tf_op jit(solution)/shard_map/slice | solution.py:56
  71.8 0.2 reshape_squeeze.7
  72.1 0.3 convolution_bitcast_fusion.4
  72.4 0.3 convolution_bitcast_fusion.5
  72.8 1.4 reshape_squeeze.8
  74.2 1.4 convolution_bitcast_fusion.3
  75.5 0.7 pad_maximum_fusion.1
  76.4 0.6 dynamic-slice
  77.6 0.1 select_reduce_fusion
  77.8 0.2 dynamic-update-slice
  78.0 4.9 %all-reduce = bf16[12]{0:T(256)(128)(2,1)S(1)} all-reduce(bf16[12]{0:T(256)(128)(2,1)S(1)} %dynamic-update-slice), channel_id=3, replica_groups=mesh['dp'=2,'expert'=16] {'dp'}, use_global_device_ids=true, to_apply=%add | all-reduce | flops 12 | bytes 48
  82.9 0.1 reshape.265
  83.0 21.8 %all-gather.2 = bf16[32,1,6]{2,1,0:T(2,128)(2,1)S(1)} all-gather(bf16[2,1,6]{2,1,0:T(2,128)(2,1)S(1)} %reshape.265), channel_id=4, replica_groups=mesh['dp'=2,'expert'=16] {'expert'}, dimensions={0}, use_global_device_ids=true | all-gather | bytes 408 | tf_op jit(solution)/shard_map/all_gather | solution.py:49
  104.9 0.7 reshape.251
  105.6 1.8 %fusion.7 = (bf16[192,128]{1,0:T(8,128)(2,1)}, bf16[1,192,128]{2,1,0:T(8,128)(2,1)S(1)}) fusion(f32[3,192,128]{2,1,0:T(8,128)} %all-reduce.3.cloned.1.call-done, f32[192]{0:T(256)} %reshape.251), kind=kLoop, calls=%fused_computation.32 | loop fusion | flops 344064 | bytes 393984 | tf_op jit(solution)/shard_map/convert_element_type | solution.py:74
  107.3 1.4 fusion.10
  108.7 0.6 fusion.1
  109.4 1.4 convert_element_type.152
  110.7 4.1 %all-to-all-start.4 = ((bf16[16,1,12]{2,1,0:T(2,128)(2,1)}), bf16[16,1,12]{2,1,0:T(2,128)(2,1)}, u32[]{:S(2)}, u32[]{:S(2)}) async-start(bf16[16,1,12]{2,1,0:T(2,128)(2,1)} %convert_element_type.152), calls=%async_computation.4 | async-start | bytes 16384 | tf_op jit(solution)/shard_map/all_to_all | solution.py:89
  114.8 2.5 %fusion = bf16[192,1792]{1,0:T(8,128)(2,1)} fusion(f32[192,1792]{1,0:T(8,128)} %fusion.10, bf16[192,128]{1,0:T(8,128)(2,1)} %get-tuple-element.61, bf16[1792,128]{0,1:T(8,128)(2,1)S(1)} %bitcast.104), kind=kOutput, calls=%fused_computation.4 | convolution fusion | flops 88768512 | bytes 2572288 | tf_op jit(solution)/shard_map/rh,dh->rd/dot_general | solution.py:78
  117.3 2.1 %reshape.247 = bf16[16,12,1792]{2,1,0:T(8,128)(2,1)} reshape(bf16[192,1792]{1,0:T(8,128)(2,1)} %fusion) | data formatting | bytes 1376256 | tf_op jit(solution)/shard_map/reshape | solution.py:87
  119.4 1.6 all-to-all-done.4
  121.0 4.5 %all-to-all-start.2 = ((bf16[16,12,1792]{2,1,0:T(8,128)(2,1)}), bf16[16,12,1792]{2,1,0:T(8,128)(2,1)}, u32[]{:S(2)}, u32[]{:S(2)}) async-start(bf16[16,12,1792]{2,1,0:T(8,128)(2,1)} %reshape.247), calls=%async_computation.2 | async-start | bytes 1835008 | tf_op jit(solution)/shard_map/all_to_all | solution.py:86
  125.5 1.3 fusion.17
  126.8 1.0 copy.162
  127.8 1.0 copy.163
  128.8 2.0 %copy.164 = bf16[1,1792,128]{2,1,0:T(8,128)(2,1)} copy(bf16[1,1792,128]{1,2,0:T(8,128)(2,1)} %bitcast.112) | data formatting | bytes 917504
  130.8 1.4 convolution_bitcast_fusion.1
  132.1 1.4 convolution_bitcast_fusion.2
  133.5 1.4 convolution_bitcast_fusion
  134.9 0.7 convert_reduce_fusion.1
  135.7 0.1 reduce_sum.53
  135.8 10.6 %all-to-all-done.2 = bf16[16,12,1792]{2,1,0:T(8,128)(2,1)} async-done(((bf16[16,12,1792]{2,1,0:T(8,128)(2,1)}), bf16[16,12,1792]{2,1,0:T(8,128)(2,1)}, u32[]{:S(2)}, u32[]{:S(2)}) %all-to-all-start.2) | async-done | bytes 688160 | tf_op jit(solution)/shard_map/all_to_all | solution.py:86
  146.3 1.3 reduce_sum.50
  147.7 0.6 transpose.14
  148.3 3.3 %all-to-all-start.3 = ((bf16[2,1,6,1792]{3,2,1,0:T(8,128)(2,1)}), bf16[2,1,6,1792]{3,2,1,0:T(8,128)(2,1)S(1)}, u32[]{:S(2)}, u32[]{:S(2)}) async-start(bf16[2,1,6,1792]{3,2,1,0:T(8,128)(2,1)} %bitcast.21), calls=%async_computation.3 | async-start | bytes 114688 | tf_op jit(solution)/shard_map/all_to_all | solution.py:95
  151.6 0.7 fusion.18
  152.4 3.3 %all-to-all-done.3 = bf16[2,1,6,1792]{3,2,1,0:T(8,128)(2,1)S(1)} async-done(((bf16[2,1,6,1792]{3,2,1,0:T(8,128)(2,1)}), bf16[2,1,6,1792]{3,2,1,0:T(8,128)(2,1)S(1)}, u32[]{:S(2)}, u32[]{:S(2)}) %all-to-all-start.3) | async-done | bytes 43040 | tf_op jit(solution)/shard_map/all_to_all | solution.py:95
  155.7 1.4 convolution_convert_fusion
  (44 shorter events, 0.5 us)
Async XLA Ops:
  7.2 2.9 %copy-start = (bf16[128,3584]{1,0:T(8,128)(2,1)S(1)}, bf16[128,3584]{1,0:T(8,128)(2,1)}, u32[]{:S(2)}) copy-start(bf16[128,3584]{1,0:T(8,128)(2,1)} %param.7) | copy-start | bytes 2752516
  7.2 3.2 %copy-start.2 = (bf16[128,3584]{1,0:T(8,128)(2,1)S(1)}, bf16[128,3584]{1,0:T(8,128)(2,1)}, u32[]{:S(2)}) copy-start(bf16[128,3584]{1,0:T(8,128)(2,1)} %param.8) | copy-start | bytes 2752516
  7.2 56.0 %all-gather.5.cloned.1.call-start = ((), (), s32[]{:S(2)}) async-start(), calls=%async_computation.6 | async-start | bytes 1462272 | tf_op jit(solution)/shard_map/all_gather | solution.py:48
  8.1 69.5 %copy-start.9 = (pred[128,8]{0,1:T(8,128)(4,1)}, pred[128,8]{0,1:T(8,128)(4,1)S(1)}, u32[]{:S(2)}) copy-start(pred[128,8]{0,1:T(8,128)(4,1)S(1)} %get-tuple-element.63) | copy-start | bytes 3076
  10.0 67.6 %copy-start.6 = (s32[128,8]{0,1:T(8,128)}, s32[128,8]{0,1:T(8,128)S(1)}, u32[]{:S(2)}) copy-start(s32[128,8]{0,1:T(8,128)S(1)} %select_add_fusion) | copy-start | bytes 12292
  10.0 9.3 %copy-start.7 = (pred[128,6]{0,1:T(8,128)(4,1)}, pred[128,6]{0,1:T(8,128)(4,1)S(1)}, u32[]{:S(2)}) copy-start(pred[128,6]{0,1:T(8,128)(4,1)S(1)} %fusion.15) | copy-start | bytes 2308
  10.0 9.4 %copy-start.3 = (bf16[1,3584,64]{1,2,0:T(8,128)(2,1)S(1)}, bf16[1,3584,64]{1,2,0:T(8,128)(2,1)}, u32[]{:S(2)}) copy-start(bf16[1,3584,64]{1,2,0:T(8,128)(2,1)} %param.13) | copy-start | bytes 1376260
  10.0 9.4 %copy-start.4 = (bf16[1,3584,64]{1,2,0:T(8,128)(2,1)S(1)}, bf16[1,3584,64]{1,2,0:T(8,128)(2,1)}, u32[]{:S(2)}) copy-start(bf16[1,3584,64]{1,2,0:T(8,128)(2,1)} %param.12) | copy-start | bytes 1376260
  19.4 86.2 %all-reduce.3.cloned.1.call-start = ((), (), s32[]{:S(2)}) async-start(), calls=%async_computation.5 | async-start | bytes 589824 | tf_op jit(solution)/shard_map/psum | solution.py:65
  74.1 2.2 %copy-start.12 = (bf16[128,8]{0,1:T(8,128)(2,1)S(1)}, bf16[128,8]{0,1:T(8,128)(2,1)}, u32[]{:S(2)}) copy-start(bf16[128,8]{0,1:T(8,128)(2,1)} %param.10) | copy-start | bytes 6148
  74.2 2.2 %copy-start.13 = (u32[32]{0:T(128)S(1)}, u32[32]{0:T(128)}, u32[]{:S(2)}) copy-start(u32[32]{0:T(128)} %constant.34) | copy-start | bytes 388
  105.6 3.2 %copy-start.1 = (f32[3,192,128]{2,1,0:T(8,128)S(1)}, f32[3,192,128]{2,1,0:T(8,128)}, u32[]{:S(2)}) copy-start(f32[3,192,128]{2,1,0:T(8,128)} %all-reduce.3.cloned.1.call-done) | copy-start | bytes 884740
  110.7 10.3 %all-to-all-start.4 = ((bf16[16,1,12]{2,1,0:T(2,128)(2,1)}), bf16[16,1,12]{2,1,0:T(2,128)(2,1)}, u32[]{:S(2)}, u32[]{:S(2)}) async-start(bf16[16,1,12]{2,1,0:T(2,128)(2,1)} %convert_element_type.152), calls=%async_computation.4 | async-start | bytes 16384 | tf_op jit(solution)/shard_map/all_to_all | solution.py:89
  121.0 25.4 %all-to-all-start.2 = ((bf16[16,12,1792]{2,1,0:T(8,128)(2,1)}), bf16[16,12,1792]{2,1,0:T(8,128)(2,1)}, u32[]{:S(2)}, u32[]{:S(2)}) async-start(bf16[16,12,1792]{2,1,0:T(8,128)(2,1)} %reshape.247), calls=%async_computation.2 | async-start | bytes 1835008 | tf_op jit(solution)/shard_map/all_to_all | solution.py:86
  127.8 3.0 %copy-start.5 = (bf16[192,128]{1,0:T(8,128)(2,1)S(1)}, bf16[192,128]{1,0:T(8,128)(2,1)}, u32[]{:S(2)}) copy-start(bf16[192,128]{1,0:T(8,128)(2,1)} %get-tuple-element.61) | copy-start | bytes 147460
  130.8 2.8 %copy-start.10 = (f32[192]{0:T(256)S(1)}, f32[192]{0:T(256)}, u32[]{:S(2)}) copy-start(f32[192]{0:T(256)} %reshape.251) | copy-start | bytes 2308
  133.5 18.1 %copy-start.11 = (pred[128,8,6]{0,1,2:T(8,128)(4,1)S(1)}, pred[128,8,6]{0,1,2:T(8,128)(4,1)}, u32[]{:S(2)}) copy-start(pred[128,8,6]{0,1,2:T(8,128)(4,1)} %fusion.17) | copy-start | bytes 18436
  133.5 22.2 %copy-start.8 = (pred[128,6]{0,1:T(8,128)(4,1)S(1)}, pred[128,6]{0,1:T(8,128)(4,1)}, u32[]{:S(2)}) copy-start(pred[128,6]{0,1:T(8,128)(4,1)} %copy-done.7) | copy-start | bytes 2308
  148.3 7.4 %all-to-all-start.3 = ((bf16[2,1,6,1792]{3,2,1,0:T(8,128)(2,1)}), bf16[2,1,6,1792]{3,2,1,0:T(8,128)(2,1)S(1)}, u32[]{:S(2)}, u32[]{:S(2)}) async-start(bf16[2,1,6,1792]{3,2,1,0:T(8,128)(2,1)} %bitcast.21), calls=%async_computation.3 | async-start | bytes 114688 | tf_op jit(solution)/shard_map/all_to_all | solution.py:95
Sparse Core Ops, SparseCore 0:
  19.5 39.6 all-gather.4
  76.4 24.1 all-reduce.2

commit v2 on v1

--- a/solution.py
+++ b/solution.py
@@ -1,10 +1,310 @@
 import jax
 import jax.numpy as jnp
 from jax import lax
+from jax.experimental import pallas as pl
+from jax.experimental.pallas import tpu as pltpu
 from jax.sharding import PartitionSpec as P
 
 HSPLIT = 16
 CAP = 6
+
+
+MESH_ID = pl.DeviceIdType.MESH
+LANES = 128
+CHIPS = 8
+Y_SLOTS, Y_GATE, Y_UP, Y_DOWN, Y_PRE, Y_SUM = range(6)
+Z0, X0, C0, SIB, RET0, COPIES = 5, 9, 13, 21, 21, 29
+
+
+def dot(left, right, left_dim, right_dim):
+    return lax.dot_general(
+        left, right, (((left_dim,), (right_dim,)), ((), ())), preferred_element_type=jnp.float32
+    )
+
+
+def exchange_kernel(
+    tok_ref,
+    cot_ref,
+    ids_ref,
+    gates_ref,
+    wg_ref,
+    wu_ref,
+    wd_ref,
+    relaid_gate_ref,
+    relaid_up_ref,
+    relaid_down_ref,
+    grad_gate_ref,
+    grad_up_ref,
+    grad_down_ref,
+    token_grad_ref,
+    gate_grad_ref,
+    slot_send,
+    slot_recv,
+    blocks,
+    w2,
+    w3,
+    pre_send,
+    pre_recv,
+    hid,
+    parts,
+    sib_parts,
+    chip_parts,
+    final_parts,
+    sum_send,
+    sum_recv,
+    send_sems,
+    recv_sems,
+):
+    dp = lax.axis_index("dp")
+    me = lax.axis_index("expert")
+    half = w2.shape[1]
+    wide = half + LANES
+    core, chip = lax.rem(me, 2), lax.div(me, 2)
+    side, lane = lax.rem(chip, 2), lax.div(chip, 2)
+
+    def member(zz, xx, cc):
+        return (zz * 2 + xx) * 2 + cc
+
+    def z_at(step):
+        return lax.rem(lane + step + 4, 4)
+
+    partner = (1 - dp, me)
+    sibling = (dp, member(lane, side, 1 - core))
+    x_other = (dp, member(lane, 1 - side, core))
+
+    def chip_at(step):
+        return (dp, lax.rem(chip + step, CHIPS) * 2 + core)
+
+    barrier = pltpu.get_barrier_semaphore()
+    for other in [partner, sibling] + [chip_at(k) for k in range(1, CHIPS)]:
+        pl.semaphore_signal(barrier, inc=1, device_id=other, device_id_type=MESH_ID)
+
+    def copy(src, dst, number, device):
+        out = pltpu.make_async_remote_copy(
+            src_ref=src,
+            dst_ref=dst,
+            send_sem=send_sems.at[number],
+            recv_sem=recv_sems.at[number],
+            device_id=device,
+            device_id_type=MESH_ID,
+        )
+        return out
+
+    tok_count = ids_ref.shape[1]
+    hits = (ids_ref[...] == 0).astype(jnp.float32)
+    hit = jnp.sum(hits, axis=0, keepdims=True)
+    earlier = (
+        lax.broadcasted_iota(jnp.int32, (tok_count, tok_count), 0)
+        < lax.broadcasted_iota(jnp.int32, (tok_count, tok_count), 1)
+    ).astype(jnp.bfloat16)
+    rank = dot(jnp.broadcast_to(hit, (16, tok_count)).astype(jnp.bfloat16), earlier, 1, 0)
+    row = lax.broadcasted_iota(jnp.int32, (16, tok_count), 0)
+    slot = rank.astype(jnp.int32)
+    named = jnp.broadcast_to(hit, (16, tok_count))
+
+    def placed(first):
+        return jnp.where(row == slot + first, named, 0.0)
+
+    pick = placed(0)
+    gate_of = jnp.sum(hits * gates_ref[...].astype(jnp.float32), axis=0, keepdims=True)
+    slot_gate = jnp.sum(pick * gate_of, axis=1, keepdims=True)
+    pick_tok = pick.astype(jnp.bfloat16)
+    pick_cot = placed(8).astype(jnp.bfloat16)
+
+    def slots_of(which):
+        cols = pl.ds(pl.multiple_of(which * half, LANES), half)
+        return dot(pick_tok, tok_ref[:, cols], 1, 0) + dot(pick_cot, cot_ref[:, cols], 1, 0)
+
+    gate_lanes = jnp.broadcast_to(slot_gate, (16, LANES))
+    slot_send[:, :half] = slots_of(1 - dp).astype(jnp.bfloat16)
+    slot_send[:, half:] = gate_lanes.astype(jnp.bfloat16)
+
+    pl.semaphore_wait(barrier, CHIPS + 1)
+    y_slots = copy(slot_send, slot_recv, Y_SLOTS, partner)
+    y_slots.start()
+    other_cols = pl.ds(pl.multiple_of((1 - dp) * half, LANES), half)
+    own_cols = pl.ds(pl.multiple_of(dp * half, LANES), half)
+    units = wg_ref.shape[0]
+    rows_g = pl.ds(pl.multiple_of(dp * units, 64), units)
+    rows_u = pl.ds(pl.multiple_of(2 * units + dp * units, 64), units)
+    y_gate = copy(wg_ref.at[:, other_cols], w2.at[rows_g, :], Y_GATE, partner)
+    y_up = copy(wu_ref.at[:, other_cols], w2.at[rows_u, :], Y_UP, partner)
+    y_down = copy(wd_ref.at[:, other_cols], w3.at[rows_g, :], Y_DOWN, partner)
+    y_gate.start()
+    y_up.start()
+    y_down.start()
+
+    own = slots_of(dp)
+    own = jnp.concatenate([own, gate_lanes], axis=1)
+    w2[rows_g, :] = wg_ref[:, own_cols]
+    w2[rows_u, :] = wu_ref[:, own_cols]
+    w3[rows_g, :] = wd_ref[:, own_cols]
+    y_slots.wait_recv()
+    got = slot_recv[...].astype(jnp.float32)
+    low = jnp.where(dp == 0, own, got)
+    high = jnp.where(dp == 0, got, own)
+    blocks[me, 0:16, :] = jnp.concatenate([low[0:8], high[0:8]], axis=0).astype(jnp.bfloat16)
+    blocks[me, 16:32, :] = jnp.concatenate([low[8:16], high[8:16]], axis=0).astype(jnp.bfloat16)
+
+    def send_block(source, number, device):
+        out = copy(blocks.at[source], blocks.at[source], number, device)
+        out.start()
+        return out
+
+    gathered = []
+    along_z = [send_block(me, Z0 + k, (dp, member(z_at(k), side, core))) for k in range(1, 4)]
+    along_x = [send_block(me, X0, x_other)]
+    on_chip = [send_block(me, C0, sibling)]
+    for k in range(1, 4):
+        along_z[k - 1].wait_recv()
+        source = member(z_at(-k), side, core)
+        along_x.append(send_block(source, X0 + k, x_other))
+        on_chip.append(send_block(source, C0 + 2 * k, sibling))
+    for k in range(4):
+        along_x[k].wait_recv()
+        source = member(z_at(-k), 1 - side, core)
+        on_chip.append(send_block(source, C0 + 2 * k + 1, sibling))
+    for out in on_chip:
+        out.wait_recv()
+    gathered = along_z + along_x + on_chip
+
+    total = blocks.shape[0] * 16
+    slot_tok = blocks[:, 0:16, 0:half].reshape(total, half)
+    slot_cot = blocks[:, 16:32, 0:half].reshape(total, half)
+    slot_gates = blocks[:, 0:16, half:wide].reshape(total, LANES).astype(jnp.float32)
+    y_gate.wait_recv()
+    y_up.wait_recv()
+    pre = dot(slot_tok, w2[...], 1, 1)
+    pre_send[:, 0 : 2 * LANES] = pre.astype(jnp.bfloat16)
+    y_down.wait_recv()
+    back = dot(slot_cot, w3[...], 1, 1)
+    pre_send[:, 2 * LANES :] = back.astype(jnp.bfloat16)
+    y_pre = copy(pre_send, pre_recv, Y_PRE, partner)
+    y_pre.start()
+    relaid_gate_ref[...] = jnp.transpose(w2[0:LANES, :])
+    relaid_up_ref[...] = jnp.transpose(w2[LANES:, :])
+    relaid_down_ref[...] = jnp.transpose(w3[...])
+    y_pre.wait_recv()
+    pre_gate = pre[:, :LANES] + pre_recv[:, :LANES].astype(jnp.float32)
+    pre_up = pre[:, LANES:] + pre_recv[:, LANES : 2 * LANES].astype(jnp.float32)
+    back_proj = back + pre_recv[:, 2 * LANES :].astype(jnp.float32)
+    sig = jax.nn.sigmoid(pre_gate)
+    activation = pre_gate * sig
+    hidden = (activation * pre_up).astype(jnp.bfloat16).astype(jnp.float32)
+    score = jnp.sum(hidden * back_proj, axis=1, keepdims=True)
+    scaled = slot_gates * back_proj
+    hid[:, :LANES] = (scaled * pre_up * sig * (1.0 + pre_gate * (1.0 - sig))).astype(jnp.bfloat16)
+    hid[:, LANES : 2 * LANES] = (scaled * activation).astype(jnp.bfloat16)
+    hid[:, 2 * LANES :] = (slot_gates * hidden).astype(jnp.bfloat16)
+
+    def put_parts(value, cols):
+        split = value.astype(jnp.bfloat16).reshape(CHIPS, 2, 16, value.shape[1])
+        parts[0, :, :, cols] = split[:, 0]
+        parts[1, :, :, cols] = split[:, 1]
+
+    put_parts(jnp.broadcast_to(score, (total, LANES)), pl.ds(half, LANES))
+    d_both = hid[:, : 2 * LANES]
+    for tile in range(half // 256):
+        cols = pl.ds(tile * 256, 256)
+        put_parts(dot(d_both, w2[:, cols], 1, 0), cols)
+    to_sibling = copy(parts.at[1 - core], sib_parts, SIB, sibling)
+    to_sibling.start()
+
+    def grads(first, last):
+        @pl.loop(first, last)
+        def _(tile):
+            cols = pl.ds(pl.multiple_of(tile * 256, 256), 256)
+            x_tile = blocks[:, 0:16, cols].reshape(total, 256)
+            y_tile = blocks[:, 16:32, cols].reshape(total, 256)
+            both = dot(x_tile, hid[:, : 2 * LANES], 0, 0)
+            grad_gate_ref[cols, :] = both[:, :LANES]
+            grad_up_ref[cols, :] = both[:, LANES:]
+            grad_down_ref[cols, :] = dot(y_tile, hid[:, 2 * LANES :], 0, 0)
+
+    grads(0, 1)
+    to_sibling.wait_recv()
+    returned = []
+    for k in range(CHIPS):
+        dest = lax.rem(chip + k, CHIPS)
+        both = parts[core, dest].astype(jnp.float32) + sib_parts[dest].astype(jnp.float32)
+        if k == 0:
+            own_sum = both
+        else:
+            chip_parts[k] = both.astype(jnp.bfloat16)
+            out = copy(chip_parts.at[k], final_parts.at[k], RET0 + k, chip_at(k))
+            out.start()
+            returned.append(out)
+    grads(1, half // 256)
+    for k in range(1, CHIPS):
+        returned[k - 1].wait_recv()
+        own_sum = own_sum + final_parts[k].astype(jnp.float32)
+    sum_send[...] = own_sum[:, :half].astype(jnp.bfloat16)
+    y_sum = copy(sum_send, sum_recv, Y_SUM, partner)
+    y_sum.start()
+    pick_mine = placed(8 * dp)
+    score_of = jnp.sum(pick_mine * own_sum[:, half:], axis=0, keepdims=True)
+    gate_grad_ref[...] = hits * score_of
+    pick_half = pick_mine.astype(jnp.bfloat16)
+    token_grad_ref[:, own_cols] = dot(pick_half, sum_send[...], 0, 0).astype(jnp.bfloat16)
+    y_sum.wait_recv()
+    token_grad_ref[:, other_cols] = dot(pick_half, sum_recv[...], 0, 0).astype(jnp.bfloat16)
+    for out in [y_slots, y_gate, y_up, y_down, y_pre, y_sum, to_sibling] + gathered + returned:
+        out.wait_send()
+
+
+def one_expert(tokens, cotangent, route_ids, gates, w_gate, w_up, w_down):
+    slabs = lax.axis_size("expert")
+    tok_count, features = tokens.shape
+    top_count = route_ids.shape[1]
+    half = features // 2
+    wide = half + LANES
+    total = slabs * 16
+    bf16, f32 = jnp.bfloat16, jnp.float32
+    vmem = pl.BlockSpec(memory_space=pltpu.VMEM)
+    outs = pl.pallas_call(
+        exchange_kernel,
+        out_shape=[jax.ShapeDtypeStruct((half, LANES), bf16)] * 3
+        + [jax.ShapeDtypeStruct((half, LANES), f32)] * 3
+        + [
+            jax.ShapeDtypeStruct((tok_count, features), bf16),
+            jax.ShapeDtypeStruct((top_count, tok_count), f32),
+        ],
+        in_specs=[vmem] * 7,
+        out_specs=[vmem] * 8,
+        scratch_shapes=[
+            pltpu.VMEM((16, wide), bf16),
+            pltpu.VMEM((16, wide), bf16),
+            pltpu.VMEM((slabs, 32, wide), bf16),
+            pltpu.VMEM((2 * LANES, half), bf16),
+            pltpu.VMEM((LANES, half), bf16),
+            pltpu.VMEM((total, 3 * LANES), bf16),
+            pltpu.VMEM((total, 3 * LANES), bf16),
+            pltpu.VMEM((total, 3 * LANES), bf16),
+            pltpu.VMEM((2, CHIPS, 16, wide), bf16),
+            pltpu.VMEM((CHIPS, 16, wide), bf16),
+            pltpu.VMEM((CHIPS, 16, wide), bf16),
+            pltpu.VMEM((CHIPS, 16, wide), bf16),
+            pltpu.VMEM((16, half), bf16),
+            pltpu.VMEM((16, half), bf16),
+            pltpu.SemaphoreType.DMA((COPIES,)),
+            pltpu.SemaphoreType.DMA((COPIES,)),
+        ],
+        compiler_params=pltpu.CompilerParams(
+            collective_id=0, has_side_effects=True, vmem_limit_bytes=48 * 2**20
+        ),
+        cost_estimate=pl.CostEstimate(
+            flops=16 * total * half * LANES, bytes_accessed=12 * 2**20, transcendentals=total * LANES
+        ),
+    )(
+        tokens,
+        cotangent,
+        route_ids.T,
+        gates.T,
+        w_gate[0].T,
+        w_up[0].T,
+        w_down[0].T,
+    )
+    return tuple(value[None] for value in outs[:6]) + (outs[6], outs[7].T)
 
 
 def shards(tokens, cotangent, route_ids, gates, w_gate, w_up, w_down):
@@ -138,4 +438,6 @@
         P(("dp", "expert"), None),
         P(("dp", "expert"), None),
     )
-    return jax.shard_map(shards, mesh=mesh, in_specs=in_specs, out_specs=out_specs, check_vma=False)
+    fits = mesh.shape["dp"] == 2 and mesh.shape["expert"] == HSPLIT
+    body = one_expert if fits else shards
+    return jax.shard_map(body, mesh=mesh, in_specs=in_specs, out_specs=out_specs, check_vma=False)

time: 165 us -> 64 us (0.39)
  blocking collectives: 54.8 us -> 0 us
  Pallas kernels: 0 us -> 51.9 us
  local copies, waits for them, and re-layouts: 43.8 us -> 10.9 us
  waiting for transfers between devices: 15.5 us -> 0 us
  between operations: 15 us -> 0.67 us
  matrix products: 12.7 us -> 0 us
  starting transfers between devices: 12 us -> 0 us
  other arithmetic: 10.1 us -> 0 us
    pallas_call x0 -> x1, Pallas kernels: none -> 51.9 us  [one_expert(): pl.pallas_call(exchange_kernel, out_shape=[jax.ShapeDtypeStruct((half, LA...]
    all_to_all x2 -> x0, blocking collectives: 28 us -> none  [the longest x1 19.7 us: shards(): lax.all_to_all(weights, 'dp', split_axis=1, concat_axis=2, tiled=True)]
    all_gather x1 -> x0, blocking collectives: 21.8 us -> none  [shards(): gate_recv = lax.all_gather(gate_all, 'expert', axis=0, tiled=False)[:, :, 0]]
    all_to_all x3 -> x0, waiting for transfers between devices: 15.5 us -> none  [the longest x1 10.6 us: shards(): lax.all_to_all(partial_value.reshape(slabs, rows, part), 'expert', split_...]
    dot_general x12 -> x0, matrix products: 12.7 us -> none  [the longest x1 2.55 us: shards(): jnp.einsum('rh,dh->rd', d_up, relaid[1], preferred_element_type=jnp.float32)]
    all_to_all x3 -> x0, starting transfers between devices: 11.9 us -> none  [the longest x1 4.53 us: shards(): lax.all_to_all(partial_value.reshape(slabs, rows, part), 'expert', split_...]
    slice x6 -> x0, local copies, waits for them, and re-layouts: 10.7 us -> none  [the longest x1 8.67 us: shards(): slot_cotan = recv[:, :, 1].reshape(-1, part)]
    all_to_all x1 -> x0, local copies, waits for them, and re-layouts: 8.53 us -> none  [shards(): lax.all_to_all(weights, 'dp', split_axis=1, concat_axis=2, tiled=True)]
  transfers between devices with their start and end apart: 5 -> 0, of which waited for: 3 -> 0; matrix products, arithmetic and copies ran while one was open for 25% -> 0% of each run, Pallas kernels for 0% -> 0%
where the time goes in v2:
time: 64 us; the launch traced here: 63.5 us
  Pallas kernels  51.9 us (81%)
  local copies, waits for them, and re-layouts  10.9 us (17%)
  between operations  0.67 us (1%)
    pallas_call x1, Pallas kernels, one_expert(): pl.pallas_call(exchange_kernel, out_shape=[jax.ShapeDtypeStruct((half, LA...  51.9 us
    unnamed x20, local copies, waits for them, and re-layouts  10.9 us

profile of v2, /device:TPU:0, one launch (start us, length us, event | category | flops | bytes accessed | tf_op | source)
XLA Modules:
  0.0 63.5 jit_solution(6071804559513706510)
XLA Ops:
  0.6 0.0 copy-start.3
  0.6 0.0 copy-start.4
  0.7 0.7 %copy-done.3 = s32[128,8]{0,1:T(8,128)S(1)} copy-done((s32[128,8]{0,1:T(8,128)S(1)}, s32[128,8]{0,1:T(8,128)}, u32[]{:S(2)}) %copy-start.3) | copy-done | bytes 4120
  1.3 0.0 copy-done.4
  1.3 0.0 copy-start
  1.3 1.0 %copy-done = bf16[1,3584,64]{1,2,0:T(8,128)(2,1)S(1)} copy-done((bf16[1,3584,64]{1,2,0:T(8,128)(2,1)S(1)}, bf16[1,3584,64]{1,2,0:T(8,128)(2,1)}, u32[]{:S(2)}) %copy-start) | copy-done | bytes 458776
  2.4 0.0 copy-start.1
  2.4 1.0 %copy-done.1 = bf16[1,3584,64]{1,2,0:T(8,128)(2,1)S(1)} copy-done((bf16[1,3584,64]{1,2,0:T(8,128)(2,1)S(1)}, bf16[1,3584,64]{1,2,0:T(8,128)(2,1)}, u32[]{:S(2)}) %copy-start.1) | copy-done | bytes 458776
  3.4 0.0 copy-start.2
  3.4 1.0 %copy-done.2 = bf16[1,3584,64]{1,2,0:T(8,128)(2,1)S(1)} copy-done((bf16[1,3584,64]{1,2,0:T(8,128)(2,1)S(1)}, bf16[1,3584,64]{1,2,0:T(8,128)(2,1)}, u32[]{:S(2)}) %copy-start.2) | copy-done | bytes 458776
  4.4 51.9 %shard_map.134 = (bf16[1792,128]{1,0:T(8,128)(2,1)S(1)}, bf16[1792,128]{1,0:T(8,128)(2,1)S(1)}, bf16[1792,128]{1,0:T(8,128)(2,1)S(1)}, f32[1792,128]{1,0:T(8,128...) custom-call(bf16[128,3584]{1,0:T(8,128)(2,1)} %tok_ref.1, ...), custom_call_target="tpu_custom_call" | custom-call | flops 939524096 | bytes 12582912 | tf_op jit(solution)/shard_map/pallas_call | solution.py:264
  56.3 0.8 %copy.23 = bf16[1,1792,128]{2,1,0:T(8,128)(2,1)} copy(bf16[1,1792,128]{2,1,0:T(8,128)(2,1)S(1)} %bitcast.23) | data formatting | bytes 917504
  57.1 0.8 %copy.24 = bf16[1,1792,128]{2,1,0:T(8,128)(2,1)} copy(bf16[1,1792,128]{2,1,0:T(8,128)(2,1)S(1)} %bitcast.22) | data formatting | bytes 917504
  57.8 0.8 %copy.25 = bf16[1,1792,128]{2,1,0:T(8,128)(2,1)} copy(bf16[1,1792,128]{2,1,0:T(8,128)(2,1)S(1)} %bitcast.21) | data formatting | bytes 917504
  58.6 0.9 %copy.26 = f32[1,1792,128]{2,1,0:T(8,128)} copy(f32[1,1792,128]{2,1,0:T(8,128)S(1)} %bitcast.20) | data formatting | bytes 1835008
  59.5 0.9 %copy.27 = f32[1,1792,128]{2,1,0:T(8,128)} copy(f32[1,1792,128]{2,1,0:T(8,128)S(1)} %bitcast.19) | data formatting | bytes 1835008
  60.4 0.0 copy-start.5
  60.5 0.9 %copy.28 = f32[1,1792,128]{2,1,0:T(8,128)} copy(f32[1,1792,128]{2,1,0:T(8,128)S(1)} %bitcast.18) | data formatting | bytes 1835008
  61.4 0.6 copy-done.5
  62.0 0.9 %copy.29 = bf16[128,3584]{1,0:T(8,128)(2,1)} copy(bf16[128,3584]{1,0:T(8,128)(2,1)S(1)} %copy-done.5) | data formatting | bytes 1835008
  62.9 0.6 copy.30
Async XLA Ops:
  0.6 0.7 %copy-start.3 = (s32[128,8]{0,1:T(8,128)S(1)}, s32[128,8]{0,1:T(8,128)}, u32[]{:S(2)}) copy-start(s32[128,8]{0,1:T(8,128)} %param.9) | copy-start | bytes 12292
  0.6 0.7 %copy-start.4 = (bf16[128,8]{0,1:T(8,128)(2,1)S(1)}, bf16[128,8]{0,1:T(8,128)(2,1)}, u32[]{:S(2)}) copy-start(bf16[128,8]{0,1:T(8,128)(2,1)} %param.10) | copy-start | bytes 6148
  1.3 1.0 %copy-start = (bf16[1,3584,64]{1,2,0:T(8,128)(2,1)S(1)}, bf16[1,3584,64]{1,2,0:T(8,128)(2,1)}, u32[]{:S(2)}) copy-start(bf16[1,3584,64]{1,2,0:T(8,128)(2,1)} %param.11) | copy-start | bytes 1376260
  2.4 1.0 %copy-start.1 = (bf16[1,3584,64]{1,2,0:T(8,128)(2,1)S(1)}, bf16[1,3584,64]{1,2,0:T(8,128)(2,1)}, u32[]{:S(2)}) copy-start(bf16[1,3584,64]{1,2,0:T(8,128)(2,1)} %param.12) | copy-start | bytes 1376260
  3.4 1.0 %copy-start.2 = (bf16[1,3584,64]{1,2,0:T(8,128)(2,1)S(1)}, bf16[1,3584,64]{1,2,0:T(8,128)(2,1)}, u32[]{:S(2)}) copy-start(bf16[1,3584,64]{1,2,0:T(8,128)(2,1)} %param.13) | copy-start | bytes 1376260
  60.4 1.5 %copy-start.5 = (bf16[128,3584]{1,0:T(8,128)(2,1)S(1)}, bf16[128,3584]{1,0:T(8,128)(2,1)}, u32[]{:S(2)}) copy-start(bf16[128,3584]{1,0:T(8,128)(2,1)} %get-tuple-element.38) | copy-start | bytes 2752516

commit v3 on v2

--- a/solution.py
+++ b/solution.py
@@ -12,8 +12,8 @@
 MESH_ID = pl.DeviceIdType.MESH
 LANES = 128
 CHIPS = 8
-Y_SLOTS, Y_GATE, Y_UP, Y_DOWN, Y_PRE, Y_SUM = range(6)
-Z0, X0, C0, SIB, RET0, COPIES = 5, 9, 13, 21, 21, 29
+Y_SLOTS, Y_GATE, Y_UP, Y_DOWN, Y_PRE, Y_SUM, Y_BACK = range(7)
+Z0, X0, C0, SIB, RX0, RZ0, COPIES = 6, 10, 14, 22, 23, 26, 30
 
 
 def dot(left, right, left_dim, right_dim):
@@ -30,13 +30,13 @@
     wg_ref,
     wu_ref,
     wd_ref,
-    relaid_gate_ref,
-    relaid_up_ref,
-    relaid_down_ref,
-    grad_gate_ref,
-    grad_up_ref,
-    grad_down_ref,
-    token_grad_ref,
+    relaid_gate_out,
+    relaid_up_out,
+    relaid_down_out,
+    grad_gate_out,
+    grad_up_out,
+    grad_down_out,
+    token_grad_out,
     gate_grad_ref,
     slot_send,
     slot_recv,
@@ -46,14 +46,27 @@
     pre_send,
     pre_recv,
     hid,
+    hid_core,
     parts,
     sib_parts,
-    chip_parts,
-    final_parts,
+    x_send,
+    x_recv,
+    z_send,
+    z_recv,
     sum_send,
     sum_recv,
+    tok_vmem,
+    cot_vmem,
+    relaid_gate_ref,
+    relaid_up_ref,
+    relaid_down_ref,
+    grad_gate_ref,
+    grad_up_ref,
+    grad_down_ref,
+    token_grad_ref,
     send_sems,
     recv_sems,
+    local_sems,
 ):
     dp = lax.axis_index("dp")
     me = lax.axis_index("expert")
@@ -90,6 +103,31 @@
         )
         return out
 
+    other_cols = pl.ds(pl.multiple_of((1 - dp) * half, LANES), half)
+    own_cols = pl.ds(pl.multiple_of(dp * half, LANES), half)
+    units = wg_ref.shape[0]
+    rows_g = pl.ds(pl.multiple_of(dp * units, 64), units)
+    rows_u = pl.ds(pl.multiple_of(2 * units + dp * units, 64), units)
+    local = [
+        pltpu.make_async_copy(source, target, local_sems.at[number])
+        for number, (source, target) in enumerate(
+            [
+                (tok_ref, tok_vmem),
+                (cot_ref, cot_vmem),
+                (wg_ref.at[:, own_cols], w2.at[rows_g, :]),
+                (wu_ref.at[:, own_cols], w2.at[rows_u, :]),
+                (wd_ref.at[:, own_cols], w3.at[rows_g, :]),
+            ]
+        )
+    ]
+    for out in local:
+        out.start()
+
+    def store(number, source, target):
+        out = pltpu.make_async_copy(source, target, local_sems.at[5 + number])
+        out.start()
+        return out
+
     tok_count = ids_ref.shape[1]
     hits = (ids_ref[...] == 0).astype(jnp.float32)
     hit = jnp.sum(hits, axis=0, keepdims=True)
@@ -113,32 +151,25 @@
 
     def slots_of(which):
         cols = pl.ds(pl.multiple_of(which * half, LANES), half)
-        return dot(pick_tok, tok_ref[:, cols], 1, 0) + dot(pick_cot, cot_ref[:, cols], 1, 0)
-
+        return dot(pick_tok, tok_vmem[:, cols], 1, 0) + dot(pick_cot, cot_vmem[:, cols], 1, 0)
+
+    y_gate = copy(wg_ref.at[:, other_cols], w2.at[rows_g, :], Y_GATE, partner)
+    y_up = copy(wu_ref.at[:, other_cols], w2.at[rows_u, :], Y_UP, partner)
+    y_down = copy(wd_ref.at[:, other_cols], w3.at[rows_g, :], Y_DOWN, partner)
+    pl.semaphore_wait(barrier, CHIPS + 1)
+    y_gate.start()
+    local[0].wait()
+    local[1].wait()
     gate_lanes = jnp.broadcast_to(slot_gate, (16, LANES))
     slot_send[:, :half] = slots_of(1 - dp).astype(jnp.bfloat16)
     slot_send[:, half:] = gate_lanes.astype(jnp.bfloat16)
-
-    pl.semaphore_wait(barrier, CHIPS + 1)
     y_slots = copy(slot_send, slot_recv, Y_SLOTS, partner)
     y_slots.start()
-    other_cols = pl.ds(pl.multiple_of((1 - dp) * half, LANES), half)
-    own_cols = pl.ds(pl.multiple_of(dp * half, LANES), half)
-    units = wg_ref.shape[0]
-    rows_g = pl.ds(pl.multiple_of(dp * units, 64), units)
-    rows_u = pl.ds(pl.multiple_of(2 * units + dp * units, 64), units)
-    y_gate = copy(wg_ref.at[:, other_cols], w2.at[rows_g, :], Y_GATE, partner)
-    y_up = copy(wu_ref.at[:, other_cols], w2.at[rows_u, :], Y_UP, partner)
-    y_down = copy(wd_ref.at[:, other_cols], w3.at[rows_g, :], Y_DOWN, partner)
-    y_gate.start()
     y_up.start()
     y_down.start()
 
     own = slots_of(dp)
     own = jnp.concatenate([own, gate_lanes], axis=1)
-    w2[rows_g, :] = wg_ref[:, own_cols]
-    w2[rows_u, :] = wu_ref[:, own_cols]
-    w3[rows_g, :] = wd_ref[:, own_cols]
     y_slots.wait_recv()
     got = slot_recv[...].astype(jnp.float32)
     low = jnp.where(dp == 0, own, got)
@@ -172,19 +203,30 @@
     slot_tok = blocks[:, 0:16, 0:half].reshape(total, half)
     slot_cot = blocks[:, 16:32, 0:half].reshape(total, half)
     slot_gates = blocks[:, 0:16, half:wide].reshape(total, LANES).astype(jnp.float32)
+    for out in local[2:]:
+        out.wait()
     y_gate.wait_recv()
     y_up.wait_recv()
     pre = dot(slot_tok, w2[...], 1, 1)
-    pre_send[:, 0 : 2 * LANES] = pre.astype(jnp.bfloat16)
-    y_down.wait_recv()
-    back = dot(slot_cot, w3[...], 1, 1)
-    pre_send[:, 2 * LANES :] = back.astype(jnp.bfloat16)
-    y_pre = copy(pre_send, pre_recv, Y_PRE, partner)
+    fore, aft = pl.ds(0, 2 * LANES), pl.ds(2 * LANES, LANES)
+    pre_send[:, fore] = pre.astype(jnp.bfloat16)
+    y_pre = copy(pre_send.at[:, fore], pre_recv.at[:, fore], Y_PRE, partner)
     y_pre.start()
     relaid_gate_ref[...] = jnp.transpose(w2[0:LANES, :])
     relaid_up_ref[...] = jnp.transpose(w2[LANES:, :])
+    y_down.wait_recv()
+    back = dot(slot_cot, w3[...], 1, 1)
+    pre_send[:, aft] = back.astype(jnp.bfloat16)
+    y_back = copy(pre_send.at[:, aft], pre_recv.at[:, aft], Y_BACK, partner)
+    y_back.start()
     relaid_down_ref[...] = jnp.transpose(w3[...])
+    stores = [
+        store(0, relaid_gate_ref, relaid_gate_out),
+        store(1, relaid_up_ref, relaid_up_out),
+        store(2, relaid_down_ref, relaid_down_out),
+    ]
     y_pre.wait_recv()
+    y_back.wait_recv()
     pre_gate = pre[:, :LANES] + pre_recv[:, :LANES].astype(jnp.float32)
     pre_up = pre[:, LANES:] + pre_recv[:, LANES : 2 * LANES].astype(jnp.float32)
     back_proj = back + pre_recv[:, 2 * LANES :].astype(jnp.float32)
@@ -193,22 +235,29 @@
     hidden = (activation * pre_up).astype(jnp.bfloat16).astype(jnp.float32)
     score = jnp.sum(hidden * back_proj, axis=1, keepdims=True)
     scaled = slot_gates * back_proj
-    hid[:, :LANES] = (scaled * pre_up * sig * (1.0 + pre_gate * (1.0 - sig))).astype(jnp.bfloat16)
-    hid[:, LANES : 2 * LANES] = (scaled * activation).astype(jnp.bfloat16)
+    d_gate = (scaled * pre_up * sig * (1.0 + pre_gate * (1.0 - sig))).astype(jnp.bfloat16)
+    d_up = (scaled * activation).astype(jnp.bfloat16)
+    by_core = jnp.concatenate([d_gate, d_up], axis=1)
+    hid[:, : 2 * LANES] = by_core
     hid[:, 2 * LANES :] = (slot_gates * hidden).astype(jnp.bfloat16)
-
-    def put_parts(value, cols):
-        split = value.astype(jnp.bfloat16).reshape(CHIPS, 2, 16, value.shape[1])
-        parts[0, :, :, cols] = split[:, 0]
-        parts[1, :, :, cols] = split[:, 1]
-
-    put_parts(jnp.broadcast_to(score, (total, LANES)), pl.ds(half, LANES))
-    d_both = hid[:, : 2 * LANES]
-    for tile in range(half // 256):
-        cols = pl.ds(tile * 256, 256)
-        put_parts(dot(d_both, w2[:, cols], 1, 0), cols)
+    by_core = by_core.reshape(CHIPS, 2, 16, 2 * LANES)
+    hid_core[0] = by_core[:, 0].reshape(total // 2, 2 * LANES)
+    hid_core[1] = by_core[:, 1].reshape(total // 2, 2 * LANES)
+    scores = jnp.broadcast_to(score, (total, LANES)).astype(jnp.bfloat16)
+    scores = scores.reshape(CHIPS, 2, 16, LANES)
+    parts[0, :, :, half:] = scores[:, 0]
+    parts[1, :, :, half:] = scores[:, 1]
+
+    def put_parts(to):
+        for tile in range(half // 256):
+            cols = pl.ds(tile * 256, 256)
+            value = dot(hid_core[to], w2[:, cols], 1, 0).astype(jnp.bfloat16)
+            parts[to, :, :, cols] = value.reshape(CHIPS, 16, 256)
+
+    put_parts(1 - core)
     to_sibling = copy(parts.at[1 - core], sib_parts, SIB, sibling)
     to_sibling.start()
+    put_parts(core)
 
     def grads(first, last):
         @pl.loop(first, last)
@@ -223,21 +272,34 @@
 
     grads(0, 1)
     to_sibling.wait_recv()
-    returned = []
-    for k in range(CHIPS):
-        dest = lax.rem(chip + k, CHIPS)
-        both = parts[core, dest].astype(jnp.float32) + sib_parts[dest].astype(jnp.float32)
-        if k == 0:
-            own_sum = both
-        else:
-            chip_parts[k] = both.astype(jnp.bfloat16)
-            out = copy(chip_parts.at[k], final_parts.at[k], RET0 + k, chip_at(k))
+    def chip_sum(dest):
+        return parts[core, dest].astype(jnp.float32) + sib_parts[dest].astype(jnp.float32)
+
+    returned, across_x, back_z = [], {}, []
+    order = (2, 1, 3, 0)
+    for k in order:
+        x_send[k] = chip_sum(z_at(k) * 2 + 1 - side).astype(jnp.bfloat16)
+        across_x[k] = copy(x_send.at[k], x_recv.at[k], RX0 + k, x_other)
+        across_x[k].start()
+        returned.append(across_x[k])
+    for k in order:
+        across_x[k].wait_recv()
+        own_sum = chip_sum(z_at(k) * 2 + side) + x_recv[k].astype(jnp.float32)
+        if k:
+            z_send[k] = own_sum.astype(jnp.bfloat16)
+            out = copy(z_send.at[k], z_recv.at[k], RZ0 + k, (dp, member(z_at(k), side, core)))
             out.start()
+            back_z.append((k, out))
             returned.append(out)
     grads(1, half // 256)
-    for k in range(1, CHIPS):
-        returned[k - 1].wait_recv()
-        own_sum = own_sum + final_parts[k].astype(jnp.float32)
+    stores += [
+        store(3, grad_gate_ref, grad_gate_out),
+        store(4, grad_up_ref, grad_up_out),
+        store(5, grad_down_ref, grad_down_out),
+    ]
+    for k, out in back_z:
+        out.wait_recv()
+        own_sum = own_sum + z_recv[k].astype(jnp.float32)
     sum_send[...] = own_sum[:, :half].astype(jnp.bfloat16)
     y_sum = copy(sum_send, sum_recv, Y_SUM, partner)
     y_sum.start()
@@ -248,8 +310,22 @@
     token_grad_ref[:, own_cols] = dot(pick_half, sum_send[...], 0, 0).astype(jnp.bfloat16)
     y_sum.wait_recv()
     token_grad_ref[:, other_cols] = dot(pick_half, sum_recv[...], 0, 0).astype(jnp.bfloat16)
-    for out in [y_slots, y_gate, y_up, y_down, y_pre, y_sum, to_sibling] + gathered + returned:
+    stores.append(store(6, token_grad_ref, token_grad_out))
+    for out in stores:
+        out.wait()
+    for out in [y_slots, y_gate, y_up, y_down, y_pre, y_back, y_sum, to_sibling] + gathered + returned:
         out.wait_send()
+
+
+def store_kernel(*refs):
+    sources, targets, sems = refs[:8], refs[8:16], refs[16]
+    stores = [
+        pltpu.make_async_copy(sources[i], targets[i], sems.at[i]) for i in range(8)
+    ]
+    for out in stores:
+        out.start()
+    for out in stores:
+        out.wait()
 
 
 def one_expert(tokens, cotangent, route_ids, gates, w_gate, w_up, w_down):
@@ -261,6 +337,7 @@
     total = slabs * 16
     bf16, f32 = jnp.bfloat16, jnp.float32
     vmem = pl.BlockSpec(memory_space=pltpu.VMEM)
+    hbm = pl.BlockSpec(memory_space=pltpu.HBM)
     outs = pl.pallas_call(
         exchange_kernel,
         out_shape=[jax.ShapeDtypeStruct((half, LANES), bf16)] * 3
@@ -269,8 +346,8 @@
             jax.ShapeDtypeStruct((tok_count, features), bf16),
             jax.ShapeDtypeStruct((top_count, tok_count), f32),
         ],
-        in_specs=[vmem] * 7,
-        out_specs=[vmem] * 8,
+        in_specs=[hbm, hbm, vmem, vmem, hbm, hbm, hbm],
+        out_specs=[hbm] * 7 + [vmem],
         scratch_shapes=[
             pltpu.VMEM((16, wide), bf16),
             pltpu.VMEM((16, wide), bf16),
@@ -280,17 +357,30 @@
             pltpu.VMEM((total, 3 * LANES), bf16),
             pltpu.VMEM((total, 3 * LANES), bf16),
             pltpu.VMEM((total, 3 * LANES), bf16),
+            pltpu.VMEM((2, total // 2, 2 * LANES), bf16),
             pltpu.VMEM((2, CHIPS, 16, wide), bf16),
             pltpu.VMEM((CHIPS, 16, wide), bf16),
-            pltpu.VMEM((CHIPS, 16, wide), bf16),
-            pltpu.VMEM((CHIPS, 16, wide), bf16),
+            pltpu.VMEM((4, 16, wide), bf16),
+            pltpu.VMEM((4, 16, wide), bf16),
+            pltpu.VMEM((4, 16, wide), bf16),
+            pltpu.VMEM((4, 16, wide), bf16),
             pltpu.VMEM((16, half), bf16),
             pltpu.VMEM((16, half), bf16),
+            pltpu.VMEM((tok_count, features), bf16),
+            pltpu.VMEM((tok_count, features), bf16),
+            pltpu.VMEM((half, LANES), bf16),
+            pltpu.VMEM((half, LANES), bf16),
+            pltpu.VMEM((half, LANES), bf16),
+            pltpu.VMEM((half, LANES), f32),
+            pltpu.VMEM((half, LANES), f32),
+            pltpu.VMEM((half, LANES), f32),
+            pltpu.VMEM((tok_count, features), bf16),
             pltpu.SemaphoreType.DMA((COPIES,)),
             pltpu.SemaphoreType.DMA((COPIES,)),
+            pltpu.SemaphoreType.DMA((12,)),
         ],
         compiler_params=pltpu.CompilerParams(
-            collective_id=0, has_side_effects=True, vmem_limit_bytes=48 * 2**20
+            collective_id=0, has_side_effects=True, vmem_limit_bytes=58 * 2**20
         ),
         cost_estimate=pl.CostEstimate(
             flops=16 * total * half * LANES, bytes_accessed=12 * 2**20, transcendentals=total * LANES
@@ -304,6 +394,15 @@
         w_up[0].T,
         w_down[0].T,
     )
+    outs = pl.pallas_call(
+        store_kernel,
+        out_shape=[jax.ShapeDtypeStruct(value.shape, value.dtype) for value in outs],
+        in_specs=[hbm] * 8,
+        out_specs=[hbm] * 8,
+        scratch_shapes=[pltpu.SemaphoreType.DMA((8,))],
+        compiler_params=pltpu.CompilerParams(vmem_limit_bytes=58 * 2**20),
+        cost_estimate=pl.CostEstimate(flops=0, bytes_accessed=10 * 2**20, transcendentals=0),
+    )(*outs)
     return tuple(value[None] for value in outs[:6]) + (outs[6], outs[7].T)
 
 

time: 64 us -> 211 us (3.30)
  Pallas kernels: 51.9 us -> 210 us
  local copies, waits for them, and re-layouts: 10.9 us -> 0 us
    pallas_call x0 -> x1, Pallas kernels: none -> 154 us  [one_expert(): pl.pallas_call(store_kernel, out_shape=[jax.ShapeDtypeStruct(value.shape,...]
    unnamed x20 -> x0, local copies, waits for them, and re-layouts: 10.9 us -> none
    pallas_call x1, Pallas kernels: 51.9 us -> 56.1 us  [one_expert(): pl.pallas_call(exchange_kernel, out_shape=[jax.ShapeDtypeStruct((half, LA...]
where the time goes in v3:
time: 211 us
  Pallas kernels  210 us (100%)
    pallas_call x1, Pallas kernels, one_expert(): pl.pallas_call(store_kernel, out_shape=[jax.ShapeDtypeStruct(value.shape,...  154 us
    pallas_call x1, Pallas kernels, one_expert(): pl.pallas_call(exchange_kernel, out_shape=[jax.ShapeDtypeStruct((half, LA...  56.1 us

profile of v3, /device:TPU:0, one launch (start us, length us, event | category | flops | bytes accessed | tf_op | source)
XLA Modules:
  0.0 210.9 jit_solution(18383223400013856700)
XLA Ops:
  0.6 56.1 %shard_map.134 = (bf16[1792,128]{1,0:T(8,128)(2,1)}, bf16[1792,128]{1,0:T(8,128)(2,1)}, bf16[1792,128]{1,0:T(8,128)(2,1)}, f32[1792,128]{1,0:T(8,128)}, f32[1792...) custom-call(bf16[128,3584]{1,0:T(8,128)(2,1)} %tok_ref.1, ...), custom_call_target="tpu_custom_call" | custom-call | flops 939524096 | bytes 12582912 | tf_op jit(solution)/shard_map/pallas_call | solution.py:341
  56.7 154.2 %shard_map.135 = (bf16[1792,128]{1,0:T(8,128)(2,1)}, bf16[1792,128]{1,0:T(8,128)(2,1)}, bf16[1792,128]{1,0:T(8,128)(2,1)}, f32[1792,128]{1,0:T(8,128)}, f32[1792...) custom-call(bf16[1792,128]{1,0:T(8,128)(2,1)} %get-tuple-element.24.refs_0_, ...), custom_call_target="tpu_custom_call" | custom-call | bytes 10485760 | tf_op jit(solution)/shard_map/pallas_call | solution.py:397

commit v4 on v3

--- a/solution.py
+++ b/solution.py
@@ -318,12 +318,20 @@
 
 
 def store_kernel(*refs):
-    sources, targets, sems = refs[:8], refs[8:16], refs[16]
+    count = len(refs) // 3
+    sources, targets, staged = refs[:count], refs[count : 2 * count], refs[2 * count : 3 * count]
+    load_sems, store_sems = refs[3 * count :]
+    loads = [
+        pltpu.make_async_copy(sources[i], staged[i], load_sems.at[i]) for i in range(count)
+    ]
     stores = [
-        pltpu.make_async_copy(sources[i], targets[i], sems.at[i]) for i in range(8)
+        pltpu.make_async_copy(staged[i], targets[i], store_sems.at[i]) for i in range(count)
     ]
-    for out in stores:
+    for out in loads:
         out.start()
+    for i in range(count):
+        loads[i].wait()
+        stores[i].start()
     for out in stores:
         out.wait()
 
@@ -399,7 +407,8 @@
         out_shape=[jax.ShapeDtypeStruct(value.shape, value.dtype) for value in outs],
         in_specs=[hbm] * 8,
         out_specs=[hbm] * 8,
-        scratch_shapes=[pltpu.SemaphoreType.DMA((8,))],
+        scratch_shapes=[pltpu.VMEM(value.shape, value.dtype) for value in outs]
+        + [pltpu.SemaphoreType.DMA((8,))] * 2,
         compiler_params=pltpu.CompilerParams(vmem_limit_bytes=58 * 2**20),
         cost_estimate=pl.CostEstimate(flops=0, bytes_accessed=10 * 2**20, transcendentals=0),
     )(*outs)

time: 211 us -> 61.6 us (0.29)
  Pallas kernels: 210 us -> 60.7 us
    pallas_call x1, Pallas kernels: 154 us -> 4.65 us  [one_expert(): pl.pallas_call(store_kernel, out_shape=[jax.ShapeDtypeStruct(value.shape,...]
where the time goes in v4:
time: 61.6 us; the launch traced here: 61.4 us
  Pallas kernels  60.7 us (99%)
  between operations  0.64 us (1%)
    pallas_call x1, Pallas kernels, one_expert(): pl.pallas_call(exchange_kernel, out_shape=[jax.ShapeDtypeStruct((half, LA...  56.1 us
    pallas_call x1, Pallas kernels, one_expert(): pl.pallas_call(store_kernel, out_shape=[jax.ShapeDtypeStruct(value.shape,...  4.65 us

profile of v4, /device:TPU:0, one launch (start us, length us, event | category | flops | bytes accessed | tf_op | source)
XLA Modules:
  0.0 61.4 jit_solution(3976606977322492705)
XLA Ops:
  0.6 56.1 %shard_map.134 = (bf16[1792,128]{1,0:T(8,128)(2,1)}, bf16[1792,128]{1,0:T(8,128)(2,1)}, bf16[1792,128]{1,0:T(8,128)(2,1)}, f32[1792,128]{1,0:T(8,128)}, f32[1792...) custom-call(bf16[128,3584]{1,0:T(8,128)(2,1)} %tok_ref.1, ...), custom_call_target="tpu_custom_call" | custom-call | flops 939524096 | bytes 12582912 | tf_op jit(solution)/shard_map/pallas_call | solution.py:349
  56.7 4.7 %shard_map.135 = (bf16[1792,128]{1,0:T(8,128)(2,1)}, bf16[1792,128]{1,0:T(8,128)(2,1)}, bf16[1792,128]{1,0:T(8,128)(2,1)}, f32[1792,128]{1,0:T(8,128)}, f32[1792...) custom-call(bf16[1792,128]{1,0:T(8,128)(2,1)} %get-tuple-element.24.refs_0_, ...), custom_call_target="tpu_custom_call" | custom-call | bytes 10485760 | tf_op jit(solution)/shard_map/pallas_call | solution.py:405
